TPU v7x, 128 devices: a whole 4x4x4 slice. The times are simulated.
128 devices in a mesh: rep: 8 (over z, y_lo), shard: 16 (over y_hi, x, core).
Axes of the slice: x: 4, y: 4 (y_hi: 2, y_lo: 2; y = y_hi * 2 + y_lo), z: 4, core: 2. Of those that a mesh axis runs over, the one named last changes fastest.
Arguments:
- tokens: bfloat16 [8, 2048, 1600], P('rep', 'shard'), may hold values from -6 to 6
- segments: int32 [8, 2048], P('rep', 'shard'), may hold values from 0 to 31, as said below
- input_gain: bfloat16 [1600], P('shard'), may hold values from 0.5 to 1.5
- attention_weight: bfloat16 [1600, 2240], P('shard'), may hold values from -0.15625 to 0.15625
- attend_out: bfloat16 [1600, 1600], P('shard'), may hold values from -0.15625 to 0.15625
- mixer_weight: bfloat16 [1600, 6400], P('shard'), may hold values from -0.15625 to 0.15625
- param_weight: bfloat16 [1600, 82], P('shard'), may hold values from -0.15625 to 0.15625
- mixer_out: bfloat16 [3200, 1600], P('shard'), may hold values from -0.109375 to 0.109375
- attend_gain: bfloat16 [1600], P('shard'), may hold values from 0.5 to 1.5
- mixer_gain: bfloat16 [1600], P('shard'), may hold values from 0.5 to 1.5
- feed_gain: bfloat16 [1600], P('shard'), may hold values from 0.5 to 1.5
- gateup_weight: bfloat16 [1600, 2, 5504], P(None, None, 'shard'), may hold values from -0.15625 to 0.15625
- down_weight: bfloat16 [5504, 1600], P('shard'), may hold values from -0.078125 to 0.078125
- decay_log: float32 [50], replicated, may hold values from -5.3 to -0.7
- step_bias: float32 [50], replicated, may hold values from -3 to -1
- skip_gain: float32 [50], replicated, may hold values from 0.5 to 1.5
- cotangent: bfloat16 [8, 2048, 1600], P('rep', 'shard'), may hold values from -6 to 6
Outputs:
- output: bfloat16 [8, 2048, 1600], P('rep', 'shard')
- grad_tokens: bfloat16 [8, 2048, 1600], P('rep', 'shard')
- grad_input_gain: float32 [1600], P('shard')
- grad_attend_weight: float32 [1600, 2240], P('shard')
- grad_attend_out: float32 [1600, 1600], P('shard')
- grad_mixer_weight: float32 [1600, 6400], P('shard')
- grad_param_weight: float32 [1600, 82], P('shard')
- grad_mixer_out: float32 [3200, 1600], P('shard')
- grad_attend_gain: float32 [1600], P('shard')
- grad_mixer_gain: float32 [1600], P('shard')
- grad_feed_gain: float32 [1600], P('shard')
- grad_gateup_weight: float32 [1600, 2, 5504], P(None, None, 'shard')
- grad_down_weight: float32 [5504, 1600], P('shard')
- grad_decay_log: float32 [50], replicated
- grad_step_bias: float32 [50], replicated
- grad_skip_gain: float32 [50], replicated
Inputs may be any that keep to these rules, and one draw needn't show every extreme that they name: `segments`: within a sequence the numbers start at 0 and never fall. Each document but a sequence's last holds 64 to 800 tokens; one sequence is a single document, and another is made of documents of exactly 64 tokens.
All inputs are finite; a program needn't handle non-finite values.
Results may differ from a plain program's by a relative error of at most 0.024.
Values may be sent and summed in bfloat16 or wider, within the bound.
No kernel may reach another device: no remote copies, remote signals or barrier semaphores. Data moves between devices by JAX's collectives and lax.ppermute only.
A program may use at most 448 MiB of HBM per device.

v0:
```python
import jax
import jax.numpy as jnp
from jax import lax
from jax.sharding import PartitionSpec as P

QUERY_HEADS = 25
HEAD_SIZE = 64
KEYVALUE_HEADS = 5
WINDOW = 1024
SH = 50
SP = 64
NS = 16
DI = 3200


def prefix(array, axis, combine, identity):
    peers, index = (lax.axis_size(axis), lax.axis_index(axis))
    everything = jax.tree.map(lambda part: lax.all_gather(part, axis), array)
    start = jax.tree.map(
        lambda part, zero: jnp.broadcast_to(jnp.asarray(zero, part.dtype), part.shape),
        array,
        identity,
    )

    def prefix_hop(k, before):
        reached = k < index
        new = combine(before, jax.tree.map(lambda part: part[k], everything))
        return jax.tree.map(lambda a, b: jnp.where(reached, a, b), new, before)

    return lax.fori_loop(0, peers, prefix_hop, start)


def entering(array, axis, combine, identity):
    peers, index = (lax.axis_size(axis), lax.axis_index(axis))
    everything = jax.tree.map(
        lambda part, kind: lax.all_gather(part.astype(kind), axis),
        array,
        (jnp.bfloat16, jnp.bfloat16),
    )
    start = jax.tree.map(
        lambda part, zero: jnp.broadcast_to(jnp.asarray(zero, part.dtype), part.shape),
        array,
        identity,
    )

    def entering_hop(k, before):
        at = peers - 1 - k
        reached = at > index
        new = combine(
            before, jax.tree.map(lambda part, own: part[at].astype(own.dtype), everything, array)
        )
        return jax.tree.map(lambda a, b: jnp.where(reached, a, b), new, before)

    return lax.fori_loop(0, peers, entering_hop, start)


def root_norm(values, gain):
    return values * lax.rsqrt(jnp.mean(values * values, axis=-1, keepdims=True) + 1e-06) * gain


def branch_sum(attend_proj, mixer_proj, attend_gain, mixer_gain):
    return root_norm(attend_proj, attend_gain) + root_norm(mixer_proj, mixer_gain)


def masked_scores(heads_of_queries, heads_of_keys, seg_query, seg_keys, offset):
    scores = jnp.einsum(
        "qkgd,skd->kgqs", heads_of_queries, heads_of_keys, preferred_element_type=jnp.float32
    ) * HEAD_SIZE ** (-0.5)
    query_places = offset + jnp.arange(heads_of_queries.shape[0], dtype=jnp.int32)
    key_places = jnp.arange(heads_of_keys.shape[0], dtype=jnp.int32)
    allowed = (
        (seg_query[:, None] == seg_keys[None, :])
        & (key_places[None, :] <= query_places[:, None])
        & (query_places[:, None] - key_places[None, :] < WINDOW)
    )
    return jnp.where(allowed, scores, -1e30)


def state_pieces(inner, columns, decay_log, step_bias, skip_gain, seg_ids, seg_before):
    count_of_rows = inner.shape[0]
    drive_in = inner[:, :DI].reshape(count_of_rows, SH, SP)
    gates = inner[:, DI:]
    b_rows = columns[:, :NS]
    c_rows = columns[:, NS : 2 * NS]
    step = jax.nn.softplus(columns[:, 2 * NS :] + step_bias)
    cumul = jnp.cumsum(-jnp.exp(decay_log) * step, axis=0)
    order = jnp.arange(count_of_rows, dtype=jnp.int32)
    linked = (order[:, None] >= order[None, :]) & (seg_ids[:, None] == seg_ids[None, :])
    linked_heads = linked[:, :, None]
    gaps = jnp.where(linked_heads, cumul[:, None, :] - cumul[None, :, :], 0.0)
    inner_prod = jnp.dot(c_rows, b_rows.T, precision=lax.Precision.HIGHEST)
    kernel = jnp.where(linked_heads, jnp.exp(gaps), 0.0) * inner_prod[:, :, None]
    drive = step[:, :, None] * drive_in
    base = (
        jnp.einsum("ijh,jhp->ihp", kernel, drive, precision=lax.Precision.HIGHEST)
        + skip_gain[None, :, None] * drive_in
    )
    alive = (seg_ids == seg_before).astype(jnp.float32)
    carry_in = alive[:, None] * jnp.exp(cumul)
    tail_keep = (seg_ids == seg_ids[count_of_rows - 1]).astype(jnp.float32)
    tail = tail_keep[:, None] * jnp.exp(cumul[count_of_rows - 1][None, :] - cumul)
    end_local = jnp.einsum("jh,jhp,jn->hpn", tail, drive, b_rows, precision=lax.Precision.HIGHEST)
    return (base, carry_in, c_rows, gates, end_local, carry_in[count_of_rows - 1])


def state_finish(pieces, entry_state):
    base, carry_in, c_rows, gates, end_local, piece_decay = pieces
    count_of_rows = base.shape[0]
    entered = base + carry_in[:, :, None] * jnp.einsum(
        "in,hpn->ihp", c_rows, entry_state, precision=lax.Precision.HIGHEST
    )
    result = entered.reshape(count_of_rows, DI) * jax.nn.silu(gates)
    return (result, piece_decay[:, None, None] * entry_state + end_local)


def chain_states(earlier, later):
    return (earlier[0] * later[0], later[0][:, None, None] * earlier[1] + later[1])


def gate_values(feed_rows, weight_gateup):
    gate_up = jnp.einsum(
        "tc,csf->tsf", feed_rows, weight_gateup, preferred_element_type=jnp.float32
    )
    gate_part = gate_up[:, 0]
    up_part = gate_up[:, 1]
    sigmoid_gate = jax.nn.sigmoid(gate_part)
    silu_gate = gate_part * sigmoid_gate
    hidden = (silu_gate * up_part).astype(jnp.bfloat16)
    return (gate_part, up_part, sigmoid_gate, silu_gate, hidden)


def gate_grads(grad_hidden, gate_part, up_part, sigmoid_gate, silu_gate):
    grad_gate = grad_hidden * up_part * (sigmoid_gate * (1.0 + gate_part * (1.0 - sigmoid_gate)))
    grad_up = grad_hidden * silu_gate
    return jnp.stack([grad_gate, grad_up], axis=1).astype(jnp.bfloat16)


def local(
    tokens,
    segments,
    input_gain,
    attention_weight,
    attend_out,
    mixer_weight,
    param_weight,
    mixer_out,
    attend_gain,
    mixer_gain,
    feed_gain,
    gateup_weight,
    down_weight,
    decay_log,
    step_bias,
    skip_gain,
    cotangent,
):
    count_of_rows = tokens.shape[1]
    tok_in = tokens[0].astype(jnp.float32)
    seg_ids = segments[0]
    grad_out = cotangent[0]
    offset = lax.axis_index("shard") * count_of_rows
    query_width = QUERY_HEADS * HEAD_SIZE
    keyvalue_width = KEYVALUE_HEADS * HEAD_SIZE
    group_width = QUERY_HEADS // KEYVALUE_HEADS
    mixer_set = (
        lax.all_gather(input_gain, "shard", axis=0, tiled=True),
        lax.all_gather(attention_weight, "shard", axis=0, tiled=True),
        lax.all_gather(attend_out, "shard", axis=0, tiled=True),
        lax.all_gather(mixer_weight, "shard", axis=0, tiled=True),
        lax.all_gather(param_weight, "shard", axis=0, tiled=True),
        lax.all_gather(mixer_out, "shard", axis=0, tiled=True),
        lax.all_gather(attend_gain, "shard", axis=0, tiled=True),
        lax.all_gather(mixer_gain, "shard", axis=0, tiled=True),
        lax.all_gather(feed_gain, "shard", axis=0, tiled=True),
    )
    (
        gain_in,
        weight_triple,
        weight_attout,
        weight_inner,
        weight_columns,
        weight_mixout,
        gain_attend,
        gain_mixer,
        gain_feed,
    ) = mixer_set
    gain_in_f = gain_in.astype(jnp.float32)
    normed = root_norm(tok_in, gain_in_f).astype(jnp.bfloat16)
    triple = jnp.dot(normed, weight_triple, preferred_element_type=jnp.float32).astype(jnp.bfloat16)
    query_rows = triple[:, :query_width]
    rows_of_keys = triple[:, query_width : query_width + keyvalue_width]
    rows_of_values = triple[:, query_width + keyvalue_width :]
    seg_small = seg_ids.astype(jnp.bfloat16)
    every_key_row, every_value_row, all_segs = (
        lax.all_gather(rows_of_keys, "shard", axis=0, tiled=True),
        lax.all_gather(rows_of_values, "shard", axis=0, tiled=True),
        lax.all_gather(seg_small, "shard", axis=0, tiled=True),
    )
    seg_query = seg_ids.astype(jnp.float32)
    seg_keys = all_segs.astype(jnp.float32)
    count_of_keys = every_key_row.shape[0]
    heads_of_queries = query_rows.reshape(count_of_rows, KEYVALUE_HEADS, group_width, HEAD_SIZE)
    heads_of_keys = every_key_row.reshape(count_of_keys, KEYVALUE_HEADS, HEAD_SIZE)
    heads_of_values = every_value_row.reshape(count_of_keys, KEYVALUE_HEADS, HEAD_SIZE)
    scores = masked_scores(heads_of_queries, heads_of_keys, seg_query, seg_keys, offset)
    top_score = jnp.max(scores, axis=-1, keepdims=True)
    shifted = jnp.exp(scores - top_score)
    totals = jnp.sum(shifted, axis=-1, keepdims=True)
    log_total = top_score + jnp.log(totals)
    soft_low = (shifted / totals).astype(jnp.bfloat16)
    attended = (
        jnp.einsum("kgqs,skd->qkgd", soft_low, heads_of_values, preferred_element_type=jnp.float32)
        .reshape(count_of_rows, query_width)
        .astype(jnp.bfloat16)
    )
    attend_proj = jnp.dot(attended, weight_attout, preferred_element_type=jnp.float32)
    mixed_in = jnp.dot(normed, weight_inner, preferred_element_type=jnp.float32)
    mixed_columns = jnp.dot(normed, weight_columns, preferred_element_type=jnp.float32)
    seg_before = lax.dynamic_index_in_dim(seg_keys, jnp.maximum(offset - 1, 0), 0, keepdims=False)
    pieces = state_pieces(
        mixed_in, mixed_columns, decay_log, step_bias, skip_gain, seg_query, seg_before
    )
    piece_decay = pieces[5]
    end_local = pieces[4]
    decay_before, enter_state = prefix(
        (piece_decay, end_local),
        "shard",
        chain_states,
        (jnp.ones_like(piece_decay), jnp.zeros_like(end_local)),
    )
    mixer_res, exit_state = state_finish(pieces, enter_state)
    mixer_low = mixer_res.astype(jnp.bfloat16)
    mixer_proj = jnp.dot(mixer_low, weight_mixout, preferred_element_type=jnp.float32)
    gain_attend_f = gain_attend.astype(jnp.float32)
    gain_mixer_f = gain_mixer.astype(jnp.float32)
    middle = tok_in + branch_sum(attend_proj, mixer_proj, gain_attend_f, gain_mixer_f)
    gain_feed_f = gain_feed.astype(jnp.float32)
    feed_in = root_norm(middle, gain_feed_f).astype(jnp.bfloat16)
    weight_gateup, weight_down = (
        lax.all_gather(gateup_weight, "shard", axis=2, tiled=True),
        lax.all_gather(down_weight, "shard", axis=0, tiled=True),
    )
    gate_part, up_part, sigmoid_gate, silu_gate, hidden = gate_values(feed_in, weight_gateup)
    result = middle + jnp.dot(hidden, weight_down, preferred_element_type=jnp.float32)
    grad_down_full = jnp.einsum("tf,td->fd", hidden, grad_out, preferred_element_type=jnp.float32)
    grad_hidden = jnp.einsum("td,fd->tf", grad_out, weight_down, preferred_element_type=jnp.float32)
    grad_gateup_low = gate_grads(grad_hidden, gate_part, up_part, sigmoid_gate, silu_gate)
    grad_gateup_full = jnp.einsum(
        "tc,tsf->csf", feed_in, grad_gateup_low, preferred_element_type=jnp.float32
    )
    grad_feed_in = jnp.einsum(
        "tsf,csf->tc", grad_gateup_low, weight_gateup, preferred_element_type=jnp.float32
    )
    own_gateup, own_down = (
        lax.psum_scatter(
            grad_gateup_full.astype(jnp.bfloat16), "shard", scatter_dimension=2, tiled=True
        ).astype(jnp.float32),
        lax.psum_scatter(
            grad_down_full.astype(jnp.bfloat16), "shard", scatter_dimension=0, tiled=True
        ).astype(jnp.float32),
    )
    norm_values, feed_pull = jax.vjp(root_norm, middle, gain_feed_f)
    middle_part, grad_feed_gain = feed_pull(grad_feed_in)
    grad_middle = grad_out.astype(jnp.float32) + middle_part
    back_triple, back_attout, back_inner, back_columns, back_mixout = (
        lax.all_gather(attention_weight, "shard", axis=0, tiled=True),
        lax.all_gather(attend_out, "shard", axis=0, tiled=True),
        lax.all_gather(mixer_weight, "shard", axis=0, tiled=True),
        lax.all_gather(param_weight, "shard", axis=0, tiled=True),
        lax.all_gather(mixer_out, "shard", axis=0, tiled=True),
    )
    branch_values, branch_pull = jax.vjp(
        branch_sum, attend_proj, mixer_proj, gain_attend_f, gain_mixer_f
    )
    grad_attproj, grad_mixproj, grad_attend_gain, grad_mixer_gain = branch_pull(grad_middle)
    grad_attproj_low = grad_attproj.astype(jnp.bfloat16)
    grad_mixproj_low = grad_mixproj.astype(jnp.bfloat16)
    grad_attout_full = jnp.einsum(
        "tq,td->qd", attended, grad_attproj_low, preferred_element_type=jnp.float32
    )
    attended_gradient = jnp.einsum(
        "td,qd->tq", grad_attproj_low, back_attout, preferred_element_type=jnp.float32
    ).astype(jnp.bfloat16)
    grad_mixout_full = jnp.einsum(
        "ti,td->id", mixer_low, grad_mixproj_low, preferred_element_type=jnp.float32
    )
    grad_mixer_res = jnp.einsum(
        "td,id->ti", grad_mixproj_low, back_mixout, preferred_element_type=jnp.float32
    )
    again_scores = masked_scores(heads_of_queries, heads_of_keys, seg_query, seg_keys, offset)
    soft_again = jnp.exp(again_scores - log_total)
    soft_again_low = soft_again.astype(jnp.bfloat16)
    head_gradient = attended_gradient.reshape(count_of_rows, KEYVALUE_HEADS, group_width, HEAD_SIZE)
    grad_soft = jnp.einsum(
        "qkgd,skd->kgqs", head_gradient, heads_of_values, preferred_element_type=jnp.float32
    )
    delta_rows = jnp.sum(soft_again * grad_soft, axis=-1, keepdims=True)
    grad_scores = (soft_again * (grad_soft - delta_rows)).astype(jnp.bfloat16)
    grad_queries = (
        (
            jnp.einsum(
                "kgqs,skd->qkgd", grad_scores, heads_of_keys, preferred_element_type=jnp.float32
            )
            * HEAD_SIZE ** (-0.5)
        )
        .reshape(count_of_rows, query_width)
        .astype(jnp.bfloat16)
    )
    grad_key_part = jnp.einsum(
        "kgqs,qkgd->skd", grad_scores, heads_of_queries, preferred_element_type=jnp.float32
    ) * HEAD_SIZE ** (-0.5)
    grad_value_part = jnp.einsum(
        "kgqs,qkgd->skd", soft_again_low, head_gradient, preferred_element_type=jnp.float32
    )
    grad_keyvalue = lax.psum_scatter(
        jnp.concatenate(
            [
                grad_key_part.reshape(count_of_rows * lax.axis_size("shard"), keyvalue_width),
                grad_value_part.reshape(count_of_rows * lax.axis_size("shard"), keyvalue_width),
            ],
            axis=1,
        ).astype(jnp.bfloat16),
        "shard",
        scatter_dimension=0,
        tiled=True,
    )
    grad_triple = jnp.concatenate([grad_queries, grad_keyvalue], axis=1)
    grad_drive = (grad_mixer_res * jax.nn.silu(pieces[3])).reshape(count_of_rows, SH, SP)
    direct_grad = jnp.einsum(
        "ih,ihp,in->hpn", pieces[1], grad_drive, pieces[2], precision=lax.Precision.HIGHEST
    )
    decay_after, later_grad = entering(
        (piece_decay, direct_grad),
        "shard",
        chain_states,
        (jnp.ones_like(piece_decay), jnp.zeros_like(direct_grad)),
    )

    def state_whole(inner, columns, decay_values, bias_values, skip_values, entry_state):
        return state_finish(
            state_pieces(
                inner, columns, decay_values, bias_values, skip_values, seg_query, seg_before
            ),
            entry_state,
        )

    state_values, state_pull = jax.vjp(
        state_whole, mixed_in, mixed_columns, decay_log, step_bias, skip_gain, enter_state
    )
    grad_inner, grad_columns, grad_decay, grad_bias, grad_skip, grad_entry = state_pull(
        (grad_mixer_res, later_grad)
    )
    grad_inner_low = grad_inner.astype(jnp.bfloat16)
    grad_columns_low = grad_columns.astype(jnp.bfloat16)
    grad_triple_full = jnp.einsum(
        "tc,tw->cw", normed, grad_triple, preferred_element_type=jnp.float32
    )
    grad_inner_full = jnp.einsum(
        "tc,tw->cw", normed, grad_inner_low, preferred_element_type=jnp.float32
    )
    grad_columns_full = jnp.einsum(
        "tc,tw->cw", normed, grad_columns_low, preferred_element_type=jnp.float32
    )
    grad_normed = jnp.einsum(
        "tw,cw->tc", grad_triple, back_triple, preferred_element_type=jnp.float32
    )
    grad_normed = grad_normed + jnp.einsum(
        "tw,cw->tc", grad_inner_low, back_inner, preferred_element_type=jnp.float32
    )
    grad_normed = grad_normed + jnp.einsum(
        "tw,cw->tc", grad_columns_low, back_columns, preferred_element_type=jnp.float32
    )
    input_values, input_pull = jax.vjp(root_norm, tok_in, gain_in_f)
    tok_part, grad_input_gain = input_pull(grad_normed)
    grad_tokens = (grad_middle + tok_part).astype(jnp.bfloat16)
    mixer_owned = (
        lax.psum_scatter(
            grad_input_gain.astype(jnp.bfloat16), "shard", scatter_dimension=0, tiled=True
        ).astype(jnp.float32),
        lax.psum_scatter(
            grad_triple_full.astype(jnp.bfloat16), "shard", scatter_dimension=0, tiled=True
        ).astype(jnp.float32),
        lax.psum_scatter(
            grad_attout_full.astype(jnp.bfloat16), "shard", scatter_dimension=0, tiled=True
        ).astype(jnp.float32),
        lax.psum_scatter(
            grad_inner_full.astype(jnp.bfloat16), "shard", scatter_dimension=0, tiled=True
        ).astype(jnp.float32),
        lax.psum_scatter(
            grad_columns_full.astype(jnp.bfloat16), "shard", scatter_dimension=0, tiled=True
        ).astype(jnp.float32),
        lax.psum_scatter(
            grad_mixout_full.astype(jnp.bfloat16), "shard", scatter_dimension=0, tiled=True
        ).astype(jnp.float32),
        lax.psum_scatter(
            grad_attend_gain.astype(jnp.bfloat16), "shard", scatter_dimension=0, tiled=True
        ).astype(jnp.float32),
        lax.psum_scatter(
            grad_mixer_gain.astype(jnp.bfloat16), "shard", scatter_dimension=0, tiled=True
        ).astype(jnp.float32),
        lax.psum_scatter(
            grad_feed_gain.astype(jnp.bfloat16), "shard", scatter_dimension=0, tiled=True
        ).astype(jnp.float32),
    )
    summed = (
        lax.psum(mixer_owned[0].astype(jnp.bfloat16), "rep").astype(jnp.float32),
        lax.psum(mixer_owned[1].astype(jnp.bfloat16), "rep").astype(jnp.float32),
        lax.psum(mixer_owned[2].astype(jnp.bfloat16), "rep").astype(jnp.float32),
        lax.psum(mixer_owned[3].astype(jnp.bfloat16), "rep").astype(jnp.float32),
        lax.psum(mixer_owned[4].astype(jnp.bfloat16), "rep").astype(jnp.float32),
        lax.psum(mixer_owned[5].astype(jnp.bfloat16), "rep").astype(jnp.float32),
        lax.psum(mixer_owned[6].astype(jnp.bfloat16), "rep").astype(jnp.float32),
        lax.psum(mixer_owned[7].astype(jnp.bfloat16), "rep").astype(jnp.float32),
        lax.psum(mixer_owned[8].astype(jnp.bfloat16), "rep").astype(jnp.float32),
        lax.psum(own_gateup.astype(jnp.bfloat16), "rep").astype(jnp.float32),
        lax.psum(own_down.astype(jnp.bfloat16), "rep").astype(jnp.float32),
    )
    head_sums = lax.psum((grad_decay, grad_bias, grad_skip), ("rep", "shard"))
    return (
        result.astype(jnp.bfloat16)[None],
        grad_tokens[None],
        summed[0],
        summed[1],
        summed[2],
        summed[3],
        summed[4],
        summed[5],
        summed[6],
        summed[7],
        summed[8],
        summed[9],
        summed[10],
        head_sums[0],
        head_sums[1],
        head_sums[2],
    )


def solution(mesh):
    placed = (
        P("rep", "shard", None),
        P("rep", "shard"),
        P("shard"),
        P("shard", None),
        P("shard", None),
        P("shard", None),
        P("shard", None),
        P("shard", None),
        P("shard"),
        P("shard"),
        P("shard"),
        P(None, None, "shard"),
        P("shard", None),
        P(),
        P(),
        P(),
        P("rep", "shard", None),
    )
    return jax.shard_map(
        local,
        mesh=mesh,
        in_specs=placed,
        out_specs=(
            P("rep", "shard", None),
            P("rep", "shard", None),
            P("shard"),
            P("shard", None),
            P("shard", None),
            P("shard", None),
            P("shard", None),
            P("shard", None),
            P("shard"),
            P("shard"),
            P("shard"),
            P(None, None, "shard"),
            P("shard", None),
            P(),
            P(),
            P(),
        ),
        check_vma=False,
    )
```

profile of v0, /device:TPU:32, one launch (start us, length us, event | category | flops | bytes accessed | tf_op | source)
XLA Modules:
  0.0 2340.6 jit_solution(6874123915950074430)
XLA Ops:
  14.9 70.3 %all-reduce.27 = (bf16[1600]{0:T(1024)(128)(2,1)S(1)}, bf16[1600]{0:T(1024)(128)(2,1)S(1)}, bf16[1600]{0:T(1024)(128)(2,1)S(1)}, bf16[1600]{0:T(1024)(128)(2,1)S(1)}) all-reduce(bf16[1600]{0:T(1024)(128)(2,1)S(1)} %dynamic-update-slice, bf16[1600]{0:T(1024)(128)(2,1)S(1)} %dynamic-update-slice.2, ...), channel_id=1, replica_groups=mesh['rep'=8,'shard'=16] {'shard'}, use_global_device_ids=true, to_apply=%add.7 | all-reduce | flops 6400 | bytes 25600
  104.2 20.9 all-gather.5
  127.0 20.9 all-gather
  151.2 63.7 %all-gather.38.cloned.1.call-done = bf16[16,100,6400]{2,1,0:T(8,128)(2,1)} async-done(((bf16[1,100,6400]{2,1,0:T(8,128)(2,1)}), bf16[16,100,6400]{2,1,0:T(8,128)(2,1)}) %all-gather.38.cloned.1.call-update) | async-done | bytes 20480016 | tf_op jit(solution)/shard_map/all_gather | solution.py:169
  272.4 20.0 all-gather.7
  302.3 21.7 all-gather.22.cloned.1.call-done
  346.2 25.8 %all-gather.20.cloned.1.call-done = bf16[2048,320]{0,1:T(8,128)(2,1)} async-done(((bf16[128,320]{0,1:T(8,128)(2,1)}), bf16[2048,320]{0,1:T(8,128)(2,1)}) %all-gather.20.cloned.1.call-update) | async-done | bytes 1310736 | tf_op jit(solution)/shard_map/all_gather | solution.py:196
  389.3 49.7 %all-gather.30.cloned.1.call-done = f32[800,64,16]{1,2,0:T(8,128)} async-done(((f32[50,64,16]{1,2,0:T(8,128)}), f32[800,64,16]{1,2,0:T(8,128)}) %all-gather.30.cloned.1.call-update) | async-done | bytes 3276816 | tf_op jit(solution)/shard_map/all_gather | solution.py:18
  474.6 47.3 %all-gather.24.cloned.1.call-done = bf16[3200,1600]{1,0:T(8,128)(2,1)} async-done(((bf16[200,1600]{1,0:T(8,128)(2,1)}), bf16[3200,1600]{1,0:T(8,128)(2,1)}) %all-gather.24.cloned.1.call-update) | async-done | bytes 10240016 | tf_op jit(solution)/shard_map/all_gather | solution.py:171
  531.6 192.5 %all-gather.26.cloned.1.call-done = bf16[1600,2,5504]{0,2,1:T(8,128)(2,1)} async-done(((bf16[1600,2,344]{0,2,1:T(8,128)(2,1)}), bf16[1600,2,5504]{0,2,1:T(8,128)(2,1)}) %all-gather.26.cloned.1.call-update) | async-done | bytes 35225616 | tf_op jit(solution)/shard_map/all_gather | solution.py:240
  724.1 20.5 fusion.127
  744.6 97.0 %all-gather.28.cloned.1.call-done = bf16[5504,1600]{1,0:T(8,128)(2,1)} async-done(((bf16[344,1600]{1,0:T(8,128)(2,1)}), bf16[5504,1600]{1,0:T(8,128)(2,1)}) %all-gather.28.cloned.1.call-update) | async-done | bytes 17612816 | tf_op jit(solution)/shard_map/all_gather | solution.py:241
  853.2 22.5 multiply_reduce_fusion.2
  943.4 21.7 fusion.7
  1007.4 28.4 %all-gather.32.cloned.1.call-done = bf16[800,64,16]{1,2,0:T(8,128)(2,1)} async-done(((bf16[50,64,16]{1,2,0:T(8,128)(2,1)}), bf16[800,64,16]{1,2,0:T(8,128)(2,1)}) %all-gather.32.cloned.1.call-update) | async-done | bytes 1638416 | tf_op jit(solution)/shard_map/all_gather | solution.py:36
  1035.7 29.3 %while.31 = (s32[]{:T(128)}, f32[50,64,16]{1,2,0:T(8,128)S(1)}, s32[]{:T(128)}, bf16[16,50]{1,0:T(8,128)(2,1)}, bf16[16,50,64,16]{2,3,1,0:T(8,128)(2,1)}, /*index=5*/s32[]{:T(128)}, s32[]{:T(128)}, s32[]{:T(128)}, s32[]{:T(128)}) while((s32[]{:T(128)}, f32[50,64,16]{1,2,0:T(8,128)S(1)}, s32[]{:T(128)}, ...), condition=%wide.region_15.16_spmd.clone, body=%wide.region_14.15_spmd.clone.sunk | while | flops 256058 | bytes 512675 | solution.py:54
  1134.8 369.9 %fusion.157 = (bf16[104,2240]{1,0:T(8,128)(2,1)S(1)}, bf16[112,1600]{1,0:T(8,128)(2,1)S(1)}, bf16[104,6400]{1,0:T(8,128)(2,1)}) fusion(bf16[1600,2240]{1,0:T(8,128)(2,1)} %convolution_convert_fusion.4, bf16[1600,1600]{1,0:T(8,128)(2,1)} %convolution_convert_fusion.5, bf16[1600,6400]{1,0:T(8,128)(2,1)} %convolution_convert_fusion.1), kind=kCustom, calls=%all-reduce-scatter.3 | all-reduce-scatter fusion | flops 17244160 | bytes 34924032
  1552.0 152.5 %all-reduce.35.cloned.1.call-done = (bf16[1600,82]{0,1:T(8,128)(2,1)}, bf16[1600,2,5504]{0,2,1:T(8,128)(2,1)}) async-done(((bf16[1600,82]{0,1:T(8,128)(2,1)}, bf16[1600,2,5504]{0,2,1:T(8,128)(2,1)}), (bf16[1600,82]{0,1:T(8,128)(2,1)}, bf16[1600,2,5504]{0,2,1:T(8,128)(2,1)})) %all-reduce.35.cloned.1.call-update) | async-done | bytes 35488016
  1707.7 143.8 %reduce-scatter.20.cloned.1.call-done = bf16[200,1600]{1,0:T(8,128)(2,1)} async-done(((bf16[3200,1600]{1,0:T(8,128)(2,1)}), bf16[200,1600]{1,0:T(8,128)(2,1)}) %reduce-scatter.20.cloned.1.call-update) | async-done | bytes 640016
  1851.5 202.1 %reduce-scatter.22.cloned.1.call-done = bf16[344,1600]{1,0:T(8,128)(2,1)} async-done(((bf16[5504,1600]{1,0:T(8,128)(2,1)}), bf16[344,1600]{1,0:T(8,128)(2,1)}) %reduce-scatter.22.cloned.1.call-update) | async-done | bytes 1100816
  2068.8 65.4 %all-reduce.25 = (f32[50]{0:T(128)}, f32[50]{0:T(128)}, f32[50]{0:T(128)}) all-reduce(f32[50]{0:T(128)S(1)} %negate_multiply_fusion, f32[50]{0:T(128)S(1)} %get-tuple-element.345, f32[50]{0:T(128)S(1)} %reduce_sum.266), channel_id=1, replica_groups=mesh['rep'=8,'shard'=16] {'rep','shard'}, use_global_device_ids=true, to_apply=%region_52.53 | all-reduce | flops 150 | bytes 1200 | tf_op jit(solution)/shard_map/psum | solution.py:418
  2150.4 67.5 %all-reduce.26 = (bf16[1600]{0:T(1024)(128)(2,1)S(1)}, bf16[1600]{0:T(1024)(128)(2,1)S(1)}, bf16[1600]{0:T(1024)(128)(2,1)S(1)}, bf16[1600]{0:T(1024)(128)(2,1)S(1)}) all-reduce(bf16[1600]{0:T(1024)(128)(2,1)S(1)} %get-tuple-element.289, bf16[1600]{0:T(1024)(128)(2,1)S(1)} %copy-done.53, ...), channel_id=6, replica_groups=mesh['rep'=8,'shard'=16] {'shard'}, use_global_device_ids=true, to_apply=%region_26.27.clone | all-reduce | flops 6400 | bytes 25600
  2220.2 31.6 %all-reduce.29 = (bf16[100]{0:T(256)(128)(2,1)S(1)}, bf16[100,82]{0,1:T(8,128)(2,1)S(1)}, bf16[100]{0:T(256)(128)(2,1)S(1)}, bf16[100]{0:T(256)(128)(2,1)S(1)}, bf16[100]{0:T(256)(128)(2,1)S(1)}) all-reduce(bf16[100]{0:T(256)(128)(2,1)S(1)} %dynamic-slice.6, ...), channel_id=1, replica_groups=mesh['rep'=8,'shard'=16] {'rep'}, use_global_device_ids=true, to_apply=%region_27.28 | all-reduce | flops 8600 | bytes 34400 | tf_op jit(solution)/shard_map/psum | solution.py:406
  2254.5 68.3 %all-reduce.37.cloned.1.call-done = (bf16[100,2240]{1,0:T(8,128)(2,1)}, bf16[100,1600]{1,0:T(8,128)(2,1)}, bf16[100,6400]{1,0:T(8,128)(2,1)}, bf16[200,1600]{1,0...) async-done(((bf16[100,2240]{1,0:T(8,128)(2,1)}, bf16[100,1600]{1,0:T(8,128)(2,1)}, bf16[100,6400]{1,0:T(8,128)(2,1)}, bf16[200,1600]{1,0:T(8,128)(2,1)}, ...) | async-done | bytes 5990416 | tf_op jit(solution)/shard_map/psum | solution.py:407
  (384 shorter events, 516.1 us)
Async XLA Ops:
  7.2 79.3 %all-gather.34.cloned.1.call-start = ((), (), s32[]{:S(2)}) async-start(), calls=%async_computation.10 | async-start | bytes 8146944 | tf_op jit(solution)/shard_map/all_gather | solution.py:167
  7.9 207.0 %all-gather.38.cloned.1.call-start = ((), (), s32[]{:S(2)}) async-start(), calls=%async_computation.12 | async-start | bytes 22630400 | tf_op jit(solution)/shard_map/all_gather | solution.py:169
  8.7 284.6 %all-gather.36.cloned.1.call-start = ((), (), s32[]{:S(2)}) async-start(), calls=%async_computation.11 | async-start | bytes 5883904 | tf_op jit(solution)/shard_map/all_gather | solution.py:168
  9.4 314.7 %all-gather.22.cloned.1.call-start = ((), (), s32[]{:S(2)}) async-start(), calls=%async_computation.4 | async-start | bytes 1392640 | tf_op jit(solution)/shard_map/all_gather | solution.py:195
  85.2 147.0 %copy-start.32 = (f32[1600]{0:T(1024)}, f32[1600]{0:T(1024)S(1)}, u32[]{:S(2)}) copy-start(f32[1600]{0:T(1024)S(1)} %convert_element_type.260) | copy-start | bytes 19204
  86.4 145.8 %copy-start.44 = (f32[128]{0:T(128)}, f32[128]{0:T(128)S(1)}, u32[]{:S(2)}) copy-start(f32[128]{0:T(128)S(1)} %fusion.129) | copy-start | bytes 1540
  104.2 267.8 %all-gather.20.cloned.1.call-start = ((), (), s32[]{:S(2)}) async-start(), calls=%async_computation.3 | async-start | bytes 1392640 | tf_op jit(solution)/shard_map/all_gather | solution.py:196
  126.3 312.7 %all-gather.30.cloned.1.call-start = ((), (), s32[]{:S(2)}) async-start(), calls=%async_computation.8 | async-start | bytes 6963200 | tf_op jit(solution)/shard_map/all_gather | solution.py:18
  249.4 272.5 %all-gather.24.cloned.1.call-start = ((), (), s32[]{:S(2)}) async-start(), calls=%async_computation.5 | async-start | bytes 11315200 | tf_op jit(solution)/shard_map/all_gather | solution.py:171
  250.2 474.0 %all-gather.26.cloned.1.call-start = ((), (), s32[]{:S(2)}) async-start(), calls=%async_computation.6 | async-start | bytes 38924288 | tf_op jit(solution)/shard_map/all_gather | solution.py:240
  250.9 590.7 %all-gather.28.cloned.1.call-start = ((), (), s32[]{:S(2)}) async-start(), calls=%async_computation.7 | async-start | bytes 19462144 | tf_op jit(solution)/shard_map/all_gather | solution.py:241
  251.7 784.1 %all-gather.32.cloned.1.call-start = ((), (), s32[]{:S(2)}) async-start(), calls=%async_computation.9 | async-start | bytes 3481600 | tf_op jit(solution)/shard_map/all_gather | solution.py:36
  251.8 209.8 %copy-start.48 = (f32[128,50]{0,1:T(8,128)}, f32[128,50]{0,1:T(8,128)S(1)}, u32[]{:S(2)}) copy-start(f32[128,50]{0,1:T(8,128)S(1)} %copy.101) | copy-start | bytes 76804
  292.8 636.0 %copy-start.43 = (f32[128,128]{1,0:T(8,128)}, f32[128,128]{1,0:T(8,128)S(1)}, u32[]{:S(2)}) copy-start(f32[128,128]{1,0:T(8,128)S(1)} %fusion.144) | copy-start | bytes 196612
  531.6 344.1 %copy-start.3 = (f32[128,1600]{0,1:T(8,128)}, f32[128,1600]{0,1:T(8,128)S(1)}, u32[]{:S(2)}) copy-start(f32[128,1600]{0,1:T(8,128)S(1)} %get-tuple-element.349) | copy-start | bytes 2457604
  985.1 143.6 %reduce-scatter.18.cloned.1.call-start = ((), (), s32[]{:S(2)}) async-start(), calls=%async_computation.13 | async-start | bytes 2785280
  1006.5 698.0 %all-reduce.35.cloned.1.call-start = ((), (), s32[]{:S(2)}) async-start(), calls=%async_computation.16 | async-start | bytes 73854976
  1081.7 769.8 %reduce-scatter.20.cloned.1.call-start = ((), (), s32[]{:S(2)}) async-start(), calls=%async_computation.14 | async-start | bytes 11315200
  1089.8 963.8 %reduce-scatter.22.cloned.1.call-start = ((), (), s32[]{:S(2)}) async-start(), calls=%async_computation.15 | async-start | bytes 19462144
  1102.7 1220.1 %all-reduce.37.cloned.1.call-start = ((), (), s32[]{:S(2)}) async-start(), calls=%async_computation.17 | async-start | bytes 12513280 | tf_op jit(solution)/shard_map/psum | solution.py:407
  1504.8 13.4 collective-permute-start
  1509.1 26.7 %collective-permute-start.3 = (bf16[60,6400]{1,0:T(8,128)(2,1)}, bf16[60,6400]{1,0:T(8,128)(2,1)}, u32[]{:S(2)}, u32[]{:S(2)}) collective-permute-start(bf16[60,6400]{1,0:T(8,128)(2,1)} %slice.74), channel_id=1, source_target_pairs={{0,1},{1,2},{2,3},{3,4},{4,5},{5,6},{6,7},{7,8},{8,9},{9,10},{10,1... | collective-permute-start | bytes 2304008
  1511.3 15.1 collective-permute-start.1
  1516.0 10.3 collective-permute-start.2
  (62 other events, 1471.7 us)
Sparse Core Ops, SparseCore 0:
  10.4 72.2 all-gather.33
  85.0 129.8 all-gather.37
  217.3 58.7 all-gather.35
  278.8 45.2 all-gather.21
  326.8 45.1 all-gather.19
  374.8 64.0 all-gather.29
  441.4 80.4 all-gather.23
  524.5 199.6 all-gather.25
  726.7 114.8 all-gather.27
  985.2 50.4 all-gather.31
  1040.3 71.9 reduce-scatter.17
  1115.7 588.7 all-reduce.34
  1708.7 142.7 reduce-scatter.19
  1855.5 198.0 reduce-scatter.21
  2057.9 264.8 all-reduce.36
where the time goes:
time: 2360 us; the launch traced here: 2340 us
  waiting for transfers between devices  1100 us (47%)
  blocking collectives  686 us (29%)
  matrix products  305 us (13%)
  local copies, waits for them, and re-layouts  112 us (5%)
  other arithmetic  111 us (5%)
    unnamed x3, blocking collectives  508 us
    unnamed x23, waiting for transfers between devices  503 us
    all_gather x1, waiting for transfers between devices, local(): lax.all_gather(gateup_weight, 'shard', axis=2, tiled=True)  192 us
    all_gather x1, waiting for transfers between devices, local(): lax.all_gather(down_weight, 'shard', axis=0, tiled=True)  97 us
    unnamed x167, local copies, waits for them, and re-layouts  94.6 us
    psum x1, waiting for transfers between devices, local(): lax.psum(mixer_owned[1].astype(jnp.bfloat16), 'rep').astype(jnp.float32)  68.3 us
    psum x1, blocking collectives, local(): head_sums = lax.psum((grad_decay, grad_bias, grad_skip), ('rep', 'shard'))  65.4 us
    all_gather x1, waiting for transfers between devices, local(): lax.all_gather(mixer_weight, 'shard', axis=0, tiled=True)  63.7 us
  transfers between devices with their start and end apart: 19, of which 13 were waited for; matrix products, arithmetic and copies ran while one was open for 31% of the time, Pallas kernels for 0%

commit v1 on v0

v1 whole, which is shorter than its diff:
```python
import jax
import jax.numpy as jnp
from jax import lax
from jax.experimental import pallas as pl
from jax.experimental.pallas import tpu as pltpu
from jax.sharding import Mesh
from jax.sharding import PartitionSpec as P

QUERY_HEADS = 25
HEAD = 64
KV_HEADS = 5
GROUP = 5
WINDOW = 1024
SH = 50
NS = 16
DI = 3200
WIDTH = 1600
FF_ROWS = 344
FF_BLOCK = 136
OUT_BLOCK = 48
RING_ROWS = 192
VMEM_LIMIT = 57 * 1024 * 1024
LENGTH = 2048
PEERS = 16
ROWS = 128
SLOTS = 4
CHUNK = 128
REP = ("z", "yl")
SHARD = ("yh", "x", "core")
SCALE = HEAD**-0.5
IN_WIDTH = 896
BF = jnp.bfloat16
F32 = jnp.float32
HI = lax.Precision.HIGHEST


def mm(a, b, ca=1, cb=0):
    return lax.dot_general(
        a.astype(BF), b.astype(BF), (((ca,), (cb,)), ((), ())), preferred_element_type=F32
    )


def mm32(a, b, ca=1, cb=0):
    return lax.dot_general(
        a, b, (((ca,), (cb,)), ((), ())), precision=HI, preferred_element_type=F32
    )


QB = 256
PARTS = WINDOW // QB + 1
SPAN = QB * PARTS
BLOCKS = LENGTH // QB


def key_parts(step):
    blocks = [step - (PARTS - 1) + j for j in range(PARTS)]
    starts = [pl.multiple_of(jnp.maximum(block, 0) * QB, QB) for block in blocks]
    return starts, [jnp.where(block < 0, 1024, 0) for block in blocks]


def allowed_parts(key_segs, query_segs, starts, missing):
    key = lax.broadcasted_iota(jnp.int32, (QB, QB), 0)
    query = lax.broadcasted_iota(jnp.int32, (QB, QB), 1)
    masks = []
    for j in range(PARTS):
        mask = key_segs[pl.ds(starts[j], QB), :] + missing[j] == query_segs
        if j == 0:
            mask = mask & (key > query)
        if j == PARTS - 1:
            mask = mask & (key <= query)
        masks.append(mask)
    return masks


def scaled(q):
    return (q.astype(BF).astype(F32) * SCALE).astype(BF)


def attend_kernel(q_ref, kv_ref, kvt_ref, key_segs, query_segs, out_ref, log_ref):
    starts, missing = key_parts(pl.program_id(0))
    masks = allowed_parts(key_segs, query_segs[...], starts, missing)
    for h in range(2):
        q = scaled(q_ref[:, HEAD * h : HEAD * (h + 1)])
        scores = []
        for j in range(PARTS):
            s = mm(kv_ref[pl.ds(starts[j], QB), :HEAD], q, 1, 1)
            scores.append(jnp.where(masks[j], s, -1e30))
        top = scores[0]
        for s in scores[1:]:
            top = jnp.maximum(top, s)
        top = jnp.max(top, axis=0, keepdims=True)
        shifted = [jnp.exp(s - top) for s in scores]
        total = shifted[0]
        for s in shifted[1:]:
            total = total + s
        total = jnp.sum(total, axis=0, keepdims=True)
        inverse = 1.0 / total
        out = jnp.zeros((HEAD, QB), F32)
        for j in range(PARTS):
            soft = (shifted[j] * inverse).astype(BF)
            out = out + mm(kvt_ref[HEAD:, pl.ds(starts[j], QB)], soft)
        for c in range(2):
            out_ref[0, c, 0, HEAD * h : HEAD * (h + 1), :] = out[:, ROWS * c : ROWS * (c + 1)].astype(BF)
        log_ref[h : h + 1, :] = top + jnp.log(total)


def attend_back_kernel(
    q_ref, g_ref, kv_ref, kvt_ref, key_segs, query_segs, log_ref, dq_ref, dkv_ref, dk_acc, dv_acc
):
    step = pl.program_id(0)
    starts, missing = key_parts(step)

    @pl.when(step == 0)
    def _():
        dk_acc[...] = jnp.zeros_like(dk_acc)
        dv_acc[...] = jnp.zeros_like(dv_acc)

    masks = allowed_parts(key_segs, query_segs[...], starts, missing)
    g_t = jnp.concatenate([g_ref[0, 0, 0], g_ref[0, 1, 0]], axis=1)
    g_all = g_t.astype(F32).T.astype(BF)
    dqs = []
    for h in range(2):
        q = scaled(q_ref[:, HEAD * h : HEAD * (h + 1)])
        g = g_all[:, HEAD * h : HEAD * (h + 1)]
        log_total = log_ref[h : h + 1, :]
        softs, grads = [], []
        delta = jnp.zeros((QB, QB), F32)
        for j in range(PARTS):
            rows = pl.ds(starts[j], QB)
            s = mm(kv_ref[rows, :HEAD], q, 1, 1)
            soft = jnp.exp(jnp.where(masks[j], s - log_total, -1e30))
            d_soft = mm(kv_ref[rows, HEAD:], g_t[HEAD * h : HEAD * (h + 1), :])
            delta = delta + soft * d_soft
            dv_acc[rows, :] += mm(soft, g)
            softs.append(soft)
            grads.append(d_soft)
        delta = jnp.sum(delta, axis=0, keepdims=True)
        dq = jnp.zeros((HEAD, QB), F32)
        for j in range(PARTS):
            rows = pl.ds(starts[j], QB)
            d_scores = (softs[j] * (grads[j] - delta)).astype(BF)
            dk_acc[rows, :] += mm(d_scores, q)
            dq = dq + mm(kvt_ref[:HEAD, rows], d_scores)
        dqs.append(dq * SCALE)
    dq_ref[...] = jnp.concatenate(dqs, axis=0).T.astype(BF)

    @pl.when(step == BLOCKS - 1)
    def _():
        dkv_ref[...] = jnp.concatenate([dk_acc[...], dv_acc[...]], axis=1).astype(BF)


def whole(*shape):
    return pl.BlockSpec(shape, lambda i: (0,) * len(shape))


def attend(projected, kv, kvt, key_segs, query_segs):
    return pl.pallas_call(
        attend_kernel,
        grid=(BLOCKS,),
        in_specs=[
            pl.BlockSpec((QB, 128), lambda i: (i, 0)),
            whole(LENGTH, 128),
            whole(128, LENGTH),
            whole(LENGTH, 1),
            pl.BlockSpec((1, QB), lambda i: (0, i)),
        ],
        out_specs=[
            pl.BlockSpec((1, 2, 1, 128, ROWS), lambda i: (i // 4, 0, i % 4, 0, 0)),
            pl.BlockSpec((8, QB), lambda i: (0, i)),
        ],
        out_shape=[
            jax.ShapeDtypeStruct((2, 2, 4, 128, ROWS), BF),
            jax.ShapeDtypeStruct((8, LENGTH), F32),
        ],
        compiler_params=pltpu.CompilerParams(vmem_limit_bytes=VMEM_LIMIT),
        cost_estimate=pl.CostEstimate(
            flops=10_000_000_000, bytes_accessed=4_000_000, transcendentals=5_300_000
        ),
        name="attend",
    )(projected, kv, kvt, key_segs, query_segs)


def attend_back(projected, g, kv, kvt, key_segs, query_segs, logs):
    return pl.pallas_call(
        attend_back_kernel,
        grid=(BLOCKS,),
        in_specs=[
            pl.BlockSpec((QB, 128), lambda i: (i, 0)),
            pl.BlockSpec((1, 2, 1, 128, ROWS), lambda i: (i // 4, 0, i % 4, 0, 0)),
            whole(LENGTH, 128),
            whole(128, LENGTH),
            whole(LENGTH, 1),
            pl.BlockSpec((1, QB), lambda i: (0, i)),
            pl.BlockSpec((8, QB), lambda i: (0, i)),
        ],
        out_specs=[
            pl.BlockSpec((QB, 128), lambda i: (i, 0)),
            whole(LENGTH, 128),
        ],
        out_shape=[
            jax.ShapeDtypeStruct((LENGTH, 128), BF),
            jax.ShapeDtypeStruct((LENGTH, 128), BF),
        ],
        scratch_shapes=[
            pltpu.VMEM((LENGTH, HEAD), F32),
            pltpu.VMEM((LENGTH, HEAD), F32),
        ],
        compiler_params=pltpu.CompilerParams(vmem_limit_bytes=VMEM_LIMIT),
        cost_estimate=pl.CostEstimate(
            flops=25_000_000_000, bytes_accessed=5_000_000, transcendentals=5_300_000
        ),
        name="attend_back",
    )(projected, g, kv, kvt, key_segs, query_segs, logs)


LANES = SLOTS * 64
CHUNKS = LENGTH // CHUNK
PAIR = 2
STEP = PAIR * CHUNK
STEPS = LENGTH // STEP


def head_selector(transposed=False):
    shape = (LANES, 8) if transposed else (8, LANES)
    head = lax.broadcasted_iota(jnp.int32, shape, 1 if transposed else 0)
    lane = lax.broadcasted_iota(jnp.int32, shape, 0 if transposed else 1)
    return (lane // 64 == head).astype(F32)


def softplus(v):
    return jnp.maximum(v, 0.0) + jnp.log1p(jnp.exp(-jnp.abs(v)))


def chunk_values(u, x_ref, bcr_ref, flags_ref, seg_col, seg_row, par_ref):
    rows = slice(CHUNK * u, CHUNK * (u + 1))
    row = lax.broadcasted_iota(jnp.int32, (CHUNK, CHUNK), 0)
    col = lax.broadcasted_iota(jnp.int32, (CHUNK, CHUNK), 1)
    linked = (row >= col) & (seg_col[rows, :] == seg_row[:, rows])
    b, c = bcr_ref[rows, :NS], bcr_ref[rows, NS : 2 * NS]
    raw = bcr_ref[rows, 2 * NS : 2 * NS + 8] + par_ref[1:2, :]
    step = softplus(raw)
    logs = step * par_ref[0:1, :]
    cum = mm32((row >= col).astype(F32), logs)
    carry = flags_ref[rows, 0:1] * jnp.exp(cum)
    tail = flags_ref[rows, 1:2] * jnp.exp(cum[CHUNK - 1 : CHUNK, :] - cum)
    wide = mm32(jnp.concatenate([step, carry, tail], axis=0), head_selector())
    step_w, carry_w, tail_w = wide[:CHUNK], wide[CHUNK : 2 * CHUNK], wide[2 * CHUNK :]
    cum_t = cum.T
    inner = mm32(c, b, 1, 1)
    decays = []
    for h in range(SLOTS):
        gap = jnp.minimum(cum[:, h : h + 1] - cum_t[h : h + 1, :], 0.0)
        decays.append(jnp.where(linked, jnp.exp(gap), 0.0))
    drive = step_w * x_ref[rows, :]
    return b, c, raw, step, logs, step_w, carry_w, tail_w, inner, decays, drive


def by_head(values):
    selector = head_selector()
    return [(values * selector[h : h + 1, :]).astype(BF) for h in range(SLOTS)]


def state_kernel(
    x_ref, z_ref, bcr_ref, flags_ref, seg_col, seg_row, par_ref, skip_ref, mixed_ref, y_ref, entry_ref, state
):
    @pl.when(pl.program_id(0) == 0)
    def _():
        state[...] = jnp.zeros_like(state)

    entry = state[...]
    for u in range(PAIR):
        rows = slice(CHUNK * u, CHUNK * (u + 1))
        b, c, _, _, _, _, carry_w, tail_w, inner, decays, drive = chunk_values(
            u, x_ref, bcr_ref, flags_ref, seg_col, seg_row, par_ref
        )
        kernels = jnp.concatenate([(d * inner).astype(BF) for d in decays], axis=1)
        drives = jnp.concatenate(by_head(drive), axis=0)
        y = mm(kernels, drives) + skip_ref[...] * x_ref[rows, :]
        ends = mm(b, tail_w * drive, 0, 0)
        entry_ref[u] = entry
        y = y + carry_w * mm(c, entry)
        entry = carry_w[CHUNK - 1 : CHUNK, :] * entry + ends
        y_ref[rows, :] = y
        z = z_ref[rows, :]
        mixed_ref[0, u, 0] = (y * z * jax.nn.sigmoid(z)).T.astype(BF)
    state[...] = entry


def state_back_kernel(
    x_ref,
    z_ref,
    bcr_ref,
    flags_ref,
    seg_col,
    seg_row,
    par_ref,
    skip_ref,
    y_ref,
    entry_ref,
    g_ref,
    dx_ref,
    dz_ref,
    dbcr_ref,
    dpar_ref,
    dskip_ref,
    d_state,
):
    @pl.when(pl.program_id(0) == 0)
    def _():
        d_state[...] = jnp.zeros_like(d_state)
        dpar_ref[...] = jnp.zeros_like(dpar_ref)
        dskip_ref[...] = jnp.zeros_like(dskip_ref)

    d_exit = d_state[...]
    for u in reversed(range(PAIR)):
        rows = slice(CHUNK * u, CHUNK * (u + 1))
        b, c, raw, step, logs, step_w, carry_w, tail_w, inner, decays, drive = chunk_values(
            u, x_ref, bcr_ref, flags_ref, seg_col, seg_row, par_ref
        )
        x, z = x_ref[rows, :], z_ref[rows, :]
        g = g_ref[0, u, 0].astype(F32).T
        sig = jax.nn.sigmoid(z)
        dy = g * z * sig
        dz_ref[rows, :] = (g * y_ref[rows, :] * (sig * (1.0 + z * (1.0 - sig)))).astype(BF)
        entry = entry_ref[u]
        c_entry = mm(c, entry)
        carried = carry_w * dy
        tailed = tail_w * drive
        piece = carry_w[CHUNK - 1 : CHUNK, :]
        dys = by_head(dy)
        kernels, cols = [], []
        row_sums = jnp.zeros((CHUNK, 8), F32)
        d_inner = jnp.zeros((CHUNK, CHUNK), F32)
        place = lax.broadcasted_iota(jnp.int32, (CHUNK, 8), 1)
        drive_low = drive.astype(BF)
        for h in range(SLOTS):
            kernel = decays[h] * inner
            d_kernel = mm(dys[h], drive_low, 1, 1)
            d_inner = d_inner + decays[h] * d_kernel
            d_gap = kernel * d_kernel
            row_sums = row_sums + jnp.where(place == h, jnp.sum(d_gap, axis=1, keepdims=True), 0.0)
            cols.append(jnp.sum(d_gap, axis=0, keepdims=True))
            kernels.append(kernel.astype(BF))
        cols = jnp.concatenate(cols + [jnp.zeros((8 - SLOTS, CHUNK), F32)], axis=0).T
        d_drive = mm(jnp.concatenate(kernels, axis=0), jnp.concatenate(dys, axis=0), 0, 0)
        b_exit = mm(b, d_exit)
        d_drive = d_drive + tail_w * b_exit
        dx_ref[rows, :] = (step_w * d_drive + skip_ref[...] * dy).astype(BF)
        dskip_ref[...] += jnp.sum(dy * x, axis=0, keepdims=True)
        ends = jnp.sum(entry * d_exit, axis=0, keepdims=True) * piece
        sums = mm32(
            jnp.concatenate(
                [d_drive * x, carried * c_entry, tailed * b_exit, jnp.broadcast_to(ends, (8, LANES))], axis=0
            ),
            head_selector(True),
        )
        d_step, from_carry, from_tail = sums[:CHUNK], sums[CHUNK : 2 * CHUNK], sums[2 * CHUNK : 3 * CHUNK]
        d_last = jnp.sum(from_tail, axis=0, keepdims=True) + sums[3 * CHUNK : 3 * CHUNK + 1]
        d_cum = row_sums - cols + from_carry - from_tail
        row = lax.broadcasted_iota(jnp.int32, (CHUNK, CHUNK), 0)
        col = lax.broadcasted_iota(jnp.int32, (CHUNK, CHUNK), 1)
        d_logs = mm32((row <= col).astype(F32), d_cum) + d_last
        d_step = d_step + d_logs * par_ref[0:1, :]
        d_raw = d_step * jax.nn.sigmoid(raw)
        dpar_ref[0:1, :] += jnp.sum(d_logs * logs, axis=0, keepdims=True)
        dpar_ref[1:2, :] += jnp.sum(d_raw, axis=0, keepdims=True)
        d_b = mm(d_inner, c, 0, 0) + mm(tailed, d_exit, 1, 1)
        d_c = mm(d_inner, b) + mm(carried, entry, 1, 1)
        dbcr_ref[rows, :] = jnp.concatenate(
            [d_b, d_c, d_raw, jnp.zeros((CHUNK, 128 - 2 * NS - 8), F32)], axis=1
        ).astype(BF)
        d_exit = piece * d_exit + mm(c, carried, 0, 0)
    d_state[...] = d_exit


def owner_block(place):
    return pl.BlockSpec(
        (1, PAIR, 1, LANES, CHUNK), lambda i: (place(i) // 4, 0, place(i) % 4, 0, 0)
    )


def state_specs(place):
    return [
        pl.BlockSpec((STEP, LANES), lambda i: (place(i), 1)),
        pl.BlockSpec((STEP, LANES), lambda i: (place(i), 2)),
        pl.BlockSpec((STEP, 128), lambda i: (place(i), 6)),
        pl.BlockSpec((STEP, 2), lambda i: (place(i), 0)),
        pl.BlockSpec((STEP, 1), lambda i: (place(i), 0)),
        pl.BlockSpec((1, STEP), lambda i: (0, place(i))),
        pl.BlockSpec((2, 8), lambda i: (0, 0)),
        pl.BlockSpec((1, LANES), lambda i: (0, 0)),
    ]


def states(projected, flags, seg_col, seg_row, par, skip):
    return pl.pallas_call(
        state_kernel,
        grid=(STEPS,),
        in_specs=state_specs(lambda i: i),
        out_specs=[
            owner_block(lambda i: i),
            pl.BlockSpec((STEP, LANES), lambda i: (i, 0)),
            pl.BlockSpec((PAIR, NS, LANES), lambda i: (i, 0, 0)),
        ],
        out_shape=[
            jax.ShapeDtypeStruct((2, 2, 4, LANES, CHUNK), BF),
            jax.ShapeDtypeStruct((LENGTH, LANES), F32),
            jax.ShapeDtypeStruct((CHUNKS, NS, LANES), F32),
        ],
        scratch_shapes=[pltpu.VMEM((NS, LANES), F32)],
        compiler_params=pltpu.CompilerParams(vmem_limit_bytes=VMEM_LIMIT),
        cost_estimate=pl.CostEstimate(flops=1_500_000_000, bytes_accessed=10_000_000, transcendentals=2_000_000),
        name="states",
    )(projected, projected, projected, flags, seg_col, seg_row, par, skip)


def states_back(projected, flags, seg_col, seg_row, par, skip, y, entry, g):
    def back(i):
        return STEPS - 1 - i

    return pl.pallas_call(
        state_back_kernel,
        grid=(STEPS,),
        in_specs=state_specs(back)
        + [
            pl.BlockSpec((STEP, LANES), lambda i: (back(i), 0)),
            pl.BlockSpec((PAIR, NS, LANES), lambda i: (back(i), 0, 0)),
            owner_block(back),
        ],
        out_specs=[
            pl.BlockSpec((STEP, LANES), lambda i: (back(i), 0)),
            pl.BlockSpec((STEP, LANES), lambda i: (back(i), 0)),
            pl.BlockSpec((STEP, 128), lambda i: (back(i), 0)),
            pl.BlockSpec((2, 8), lambda i: (0, 0)),
            pl.BlockSpec((1, LANES), lambda i: (0, 0)),
        ],
        out_shape=[
            jax.ShapeDtypeStruct((LENGTH, LANES), BF),
            jax.ShapeDtypeStruct((LENGTH, LANES), BF),
            jax.ShapeDtypeStruct((LENGTH, 128), BF),
            jax.ShapeDtypeStruct((2, 8), F32),
            jax.ShapeDtypeStruct((1, LANES), F32),
        ],
        scratch_shapes=[pltpu.VMEM((NS, LANES), F32)],
        compiler_params=pltpu.CompilerParams(vmem_limit_bytes=VMEM_LIMIT),
        cost_estimate=pl.CostEstimate(flops=4_000_000_000, bytes_accessed=12_000_000, transcendentals=3_000_000),
        name="states_back",
    )(projected, projected, projected, flags, seg_col, seg_row, par, skip, y, entry, g)


def once(*shape):
    return pl.BlockSpec(shape, lambda i: (0,) * len(shape), pipeline_mode=pl.Buffered(1))


def place_kernel(where_ref, *refs):
    *blocks, out_ref = refs
    for h in range(2):
        near, right, far_top, far_low, left = blocks[5 * h : 5 * h + 5]
        half = lax.rem(where_ref[0] + h, 2) * 4
        spots = [half + lax.rem(where_ref[1] + k, 4) for k in range(4)]
        out_ref[spots[0]] = near[...]
        out_ref[spots[1]] = right[...]
        out_ref[spots[2], :64] = far_top[...]
        out_ref[spots[2], 64:] = far_low[...]
        out_ref[spots[3]] = left[...]


def place(where, blocks):
    return pl.pallas_call(
        place_kernel,
        grid=(1,),
        in_specs=[pl.BlockSpec(memory_space=pltpu.SMEM)] + [once(*v.shape) for v in blocks],
        out_specs=once(8, ROWS + 16, WIDTH),
        out_shape=jax.ShapeDtypeStruct((8, ROWS + 16, WIDTH), BF),
        compiler_params=pltpu.CompilerParams(vmem_limit_bytes=VMEM_LIMIT),
        cost_estimate=pl.CostEstimate(flops=0, bytes_accessed=9_000_000, transcendentals=0),
        name="place",
    )(where, *blocks)


def spread_kernel(attention_ref, mixer_ref, param_ref, out_ref):
    attention, mixer, param = attention_ref[...], mixer_ref[...], param_ref[...]

    def empty(width):
        return jnp.zeros((100, width), BF)

    for s in range(PEERS):
        group, pair = s // 3, s % 3
        if s == 15:
            parts = [empty(256)]
        else:
            at = 64 * (5 * group + 2 * pair)
            width = 128 if pair < 2 else 64
            parts = [attention[:, at : at + width]] + [empty(128 - width)] * (pair == 2)
            parts += [attention[:, at : at + 64] for at in (1600 + 64 * group, 1920 + 64 * group)]
        for side in (0, DI):
            parts.append(mixer[:, side + 192 * s : side + 192 * (s + 1)])
            at = side + 48 * 64 + 64 * s
            parts.append(mixer[:, at : at + 64] if s < 2 else empty(64))
        parts += [param[:, : 2 * NS], param[:, 2 * NS + 3 * s : 2 * NS + 3 * (s + 1)]]
        parts.append(param[:, 80 + s : 81 + s] if s < 2 else empty(1))
        parts.append(empty(128 - 2 * NS - SLOTS))
        out_ref[s] = jnp.concatenate(parts, axis=1)


def spread_inputs(attention, mixer, param):
    return pl.pallas_call(
        spread_kernel,
        grid=(1,),
        in_specs=[once(*v.shape) for v in (attention, mixer, param)],
        out_specs=once(PEERS, 100, IN_WIDTH),
        out_shape=jax.ShapeDtypeStruct((PEERS, 100, IN_WIDTH), BF),
        compiler_params=pltpu.CompilerParams(vmem_limit_bytes=VMEM_LIMIT),
        cost_estimate=pl.CostEstimate(flops=0, bytes_accessed=5_000_000, transcendentals=0),
        name="spread",
    )(attention, mixer, param)


def in_order(core, mine, other):
    first = jnp.where(core == 0, mine, other)
    second = jnp.where(core == 0, other, mine)
    return first, second


def project_kernel(core_ref, mine_ref, other_ref, gain_ref, weight_ref, normed_ref, out_ref, kv_ref, kvt_ref):
    mine, other = mine_ref[0, :ROWS, :].astype(F32), other_ref[0, :ROWS, :].astype(F32)
    tok = jnp.concatenate(in_order(core_ref[0], mine, other), axis=0)
    scale = lax.rsqrt(jnp.mean(tok * tok, axis=-1, keepdims=True) + 1e-06)
    normed = (tok * scale * gain_ref[...]).astype(BF)
    normed_ref[...] = normed
    projected = mm(normed, weight_ref[...])
    out_ref[...] = projected
    kv = projected[:, 128:256]
    kv_ref[...] = kv.astype(BF)
    kvt_ref[...] = kv.T.astype(BF)


def project(core, mine, other, gain, weight):
    return pl.pallas_call(
        project_kernel,
        grid=(8,),
        in_specs=[
            pl.BlockSpec(memory_space=pltpu.SMEM),
            pl.BlockSpec((1, ROWS + 16, WIDTH), lambda i: (i, 0, 0)),
            pl.BlockSpec((1, ROWS + 16, WIDTH), lambda i: (i, 0, 0)),
            once(1, WIDTH),
            once(WIDTH, IN_WIDTH),
        ],
        out_specs=[
            pl.BlockSpec((2 * ROWS, WIDTH), lambda i: (i, 0)),
            pl.BlockSpec((2 * ROWS, IN_WIDTH), lambda i: (i, 0)),
            pl.BlockSpec((2 * ROWS, 128), lambda i: (i, 0)),
            pl.BlockSpec((128, 2 * ROWS), lambda i: (0, i)),
        ],
        out_shape=[
            jax.ShapeDtypeStruct((LENGTH, WIDTH), BF),
            jax.ShapeDtypeStruct((LENGTH, IN_WIDTH), F32),
            jax.ShapeDtypeStruct((LENGTH, 128), BF),
            jax.ShapeDtypeStruct((128, LENGTH), BF),
        ],
        compiler_params=pltpu.CompilerParams(vmem_limit_bytes=VMEM_LIMIT),
        cost_estimate=pl.CostEstimate(
            flops=8_000_000_000, bytes_accessed=24_000_000, transcendentals=0
        ),
        name="project",
    )(core, mine, other, gain, weight)


def store_parts(refs, values):
    for ref, (start, stop) in zip(refs, ((0, 128), (128, 256), (256, 320), (320, 384), (384, 512))):
        ref[...] = values[start:stop].astype(BF)


def feed_kernel(*refs):
    feeds, grads, gate_ups, downs = refs[:5], refs[5:10], refs[10:14], refs[14:18]
    feed_ref, grad_ref, hidden_ref, d_gate_up_ref = refs[18:22]
    for parts, target in ((feeds, feed_ref), (grads, grad_ref)):
        at = 0
        for part in parts:
            target[at : at + part.shape[0], :] = part[...]
            at += part.shape[0]
    feed, grad = feed_ref[...], grad_ref[...]
    out = jnp.zeros((512, WIDTH), F32)
    d_feed = jnp.zeros((512, WIDTH), F32)
    for b in range(4):
        gate_up = mm(feed, gate_ups[b][...], 1, 1)
        d_hidden = mm(grad, downs[b][...], 1, 1)
        gate, up = gate_up[:, :FF_ROWS], gate_up[:, FF_ROWS:]
        sigmoid = jax.nn.sigmoid(gate)
        silu = gate * sigmoid
        hidden = (silu * up).astype(BF)
        d_gate = d_hidden * up * (sigmoid * (1.0 + gate * (1.0 - sigmoid)))
        d_gate_up = jnp.concatenate([d_gate, d_hidden * silu], axis=1).astype(BF)
        hidden_ref[b] = hidden
        d_gate_up_ref[b] = d_gate_up
        out = out + mm(hidden, downs[b][...])
        d_feed = d_feed + mm(d_gate_up, gate_ups[b][...])
    store_parts(refs[22:27], out)
    store_parts(refs[27:32], d_feed)


def feed_forward(feeds, grads, gate_ups, downs):
    parts = [(ROWS, WIDTH), (ROWS, WIDTH), (64, WIDTH), (64, WIDTH), (ROWS, WIDTH)]
    shapes = [(512, WIDTH)] * 2 + [(4, 512, FF_ROWS), (4, 512, 2 * FF_ROWS)] + parts + parts
    return pl.pallas_call(
        feed_kernel,
        grid=(1,),
        in_specs=[once(*v.shape) for v in (*feeds, *grads, *gate_ups, *downs)],
        out_specs=[once(*shape) for shape in shapes],
        out_shape=[jax.ShapeDtypeStruct(shape, BF) for shape in shapes],
        compiler_params=pltpu.CompilerParams(vmem_limit_bytes=VMEM_LIMIT),
        cost_estimate=pl.CostEstimate(
            flops=25_000_000_000, bytes_accessed=28_000_000, transcendentals=700_000
        ),
        name="feed_forward",
    )(*feeds, *grads, *gate_ups, *downs)


def feed_grads_kernel(feed_ref, grad_ref, hidden_ref, d_gate_up_ref, near_ref, far_ref):
    for b, out_ref in enumerate((near_ref, far_ref)):
        gate_up = mm(d_gate_up_ref[b], feed_ref[...], 0, 0)
        down = mm(hidden_ref[b], grad_ref[...], 0, 0)
        empty = jnp.zeros((8 * FF_BLOCK - 3 * FF_ROWS, WIDTH), F32)
        together = jnp.concatenate([gate_up, down, empty], axis=0).astype(BF)
        for i in range(8):
            out_ref[i] = together[FF_BLOCK * i : FF_BLOCK * (i + 1)]


def feed_grads(half, feed, grad, hidden, d_gate_up):
    return pl.pallas_call(
        feed_grads_kernel,
        grid=(1,),
        in_specs=[
            once(512, WIDTH),
            once(512, WIDTH),
            pl.BlockSpec((2, 512, FF_ROWS), lambda i: (half, 0, 0), pipeline_mode=pl.Buffered(1)),
            pl.BlockSpec((2, 512, 2 * FF_ROWS), lambda i: (half, 0, 0), pipeline_mode=pl.Buffered(1)),
        ],
        out_specs=[once(8, FF_BLOCK, WIDTH)] * 2,
        out_shape=[jax.ShapeDtypeStruct((8, FF_BLOCK, WIDTH), BF)] * 2,
        compiler_params=pltpu.CompilerParams(vmem_limit_bytes=VMEM_LIMIT),
        cost_estimate=pl.CostEstimate(
            flops=5_000_000_000, bytes_accessed=12_000_000, transcendentals=0
        ),
        name="feed_grads",
    )(feed, grad, hidden, d_gate_up)


def in_grads_kernel(normed_ref, *refs):
    *parts, weight_ref, small_ref, out_ref, acc = refs
    step = pl.program_id(0)

    @pl.when(step == 0)
    def _():
        acc[...] = jnp.zeros_like(acc)

    acc[...] += mm(normed_ref[...], jnp.concatenate([part[...] for part in parts], axis=1), 0, 0)

    @pl.when(step == 7)
    def _():
        width = acc.shape[1]
        product = acc[...] * weight_ref[...].astype(F32)
        gain = mm32(jnp.ones((8, width), F32), product, 1, 1)[:1]
        for s in range(PEERS):
            own_gain = jnp.pad(gain[:, 100 * s : 100 * (s + 1)], ((0, 0), (width - 128, 28)))
            out_ref[s] = jnp.concatenate(
                [acc[100 * s : 100 * (s + 1), :], small_ref[s : s + 1, :] + own_gain, jnp.zeros((3, width), F32)],
                axis=0,
            ).astype(BF)


def projected_specs():
    return [
        pl.BlockSpec((256, 128), lambda i: (i, 0)),
        pl.BlockSpec((256, 128), lambda i: (i, 0)),
        pl.BlockSpec((256, 256), lambda i: (i, 0)),
        pl.BlockSpec((256, 256), lambda i: (i, 0)),
        pl.BlockSpec((256, 128), lambda i: (i, 0)),
    ]


def in_grads(normed, parts, weight, small):
    width = weight.shape[1]
    return pl.pallas_call(
        in_grads_kernel,
        grid=(8,),
        in_specs=[pl.BlockSpec((256, WIDTH), lambda i: (i, 0))]
        + [pl.BlockSpec((256, part.shape[1]), lambda i: (i, 0)) for part in parts]
        + [once(WIDTH, width), once(PEERS, width)],
        out_specs=once(PEERS, 104, width),
        out_shape=jax.ShapeDtypeStruct((PEERS, 104, width), BF),
        scratch_shapes=[pltpu.VMEM((WIDTH, width), F32)],
        compiler_params=pltpu.CompilerParams(vmem_limit_bytes=VMEM_LIMIT),
        cost_estimate=pl.CostEstimate(
            flops=10 * LENGTH * width * 1000, bytes_accessed=14_000_000, transcendentals=0
        ),
        name="in_grads",
    )(normed, *parts, weight, small)


def d_normed_kernel(core_ref, q_ref, kv_ref, x_ref, z_ref, bcr_ref, weight_ref, kept_ref, sent_ref):
    parts = [q_ref[...], kv_ref[...], x_ref[...], z_ref[...], bcr_ref[...]]
    d_normed = mm(jnp.concatenate(parts, axis=1), weight_ref[...], 1, 1)
    kept, sent = in_order(core_ref[0], d_normed[:ROWS], d_normed[ROWS:])
    kept_ref[0] = kept.astype(BF)
    sent_ref[0] = sent.astype(BF)


def d_normed_parts(core, d_parts, weight):
    return pl.pallas_call(
        d_normed_kernel,
        grid=(8,),
        in_specs=[pl.BlockSpec(memory_space=pltpu.SMEM)] + projected_specs() + [once(WIDTH, IN_WIDTH)],
        out_specs=[pl.BlockSpec((1, ROWS, WIDTH), lambda i: (i, 0, 0))] * 2,
        out_shape=[jax.ShapeDtypeStruct((8, ROWS, WIDTH), BF)] * 2,
        compiler_params=pltpu.CompilerParams(vmem_limit_bytes=VMEM_LIMIT),
        cost_estimate=pl.CostEstimate(
            flops=8_000_000_000, bytes_accessed=13_000_000, transcendentals=0
        ),
        name="d_normed",
    )(core, *d_parts, weight)


def rep_spots(z_ref, pieces):
    near, right, far_top, far_low, left = pieces
    spots = [2 * lax.rem(z_ref[0] + k, 4) for k in range(4)]
    pairs = [(spots[0], near), (spots[1], right), (spots[3], left)]
    single = [(spots[2], far_top[...]), (spots[2] + 1, far_low[...])]
    return single + [(spot + yl, pair[yl]) for spot, pair in pairs for yl in range(2)]


def collect_kernel(z_ref, *refs):
    pieces, refs = refs[:5], refs[5:]
    heads_ref, attention_ref, mixer_ref, param_ref, low_states_ref, low_heads_ref, states_ref = refs
    for spot, block in rep_spots(z_ref, pieces):
        for i in range(2):
            states_ref[2 * spot + i] = block[i]
    shared = jnp.zeros((104, 128), F32)
    low_states_ref[...] = jnp.zeros_like(low_states_ref)
    low_heads_ref[...] = jnp.zeros_like(low_heads_ref)
    for s in range(PEERS):
        tile = heads_ref[s].astype(F32)
        low_heads_ref[s : s + 1, :] = tile[100:101, :]
        if s < 15:
            width = 128 if s % 3 < 2 else 64
            at = 64 * (5 * (s // 3) + 2 * (s % 3))
            attention_ref[:, at : at + width] = tile[:100, :width]
        tile = states_ref[s].astype(F32)
        low_states_ref[s : s + 1, :] = tile[100:101, :]
        for side in range(2):
            part = tile[:100, 256 * side : 256 * (side + 1)]
            at = DI * side + 192 * s
            mixer_ref[:, at : at + 192] = part[:, :192]
            if s < 2:
                at = DI * side + 48 * 64 + 64 * s
                mixer_ref[:, at : at + 64] = part[:, 192:]
        raw = tile[:, 512:]
        shared = shared + raw
        at = 2 * NS + 3 * s
        param_ref[:, at : at + 3] = raw[:100, 2 * NS : 2 * NS + 3]
        if s < 2:
            param_ref[:, 80 + s : 81 + s] = raw[:100, 2 * NS + 3 : 2 * NS + 4]
    param_ref[:, : 2 * NS] = shared[:100, : 2 * NS]
    for k in range(KV_HEADS):
        kv = sum(heads_ref[3 * k + j].astype(F32)[:100, 128:] for j in range(3))
        attention_ref[:, 1600 + 64 * k : 1664 + 64 * k] = kv[:, :64]
        attention_ref[:, 1920 + 64 * k : 1984 + 64 * k] = kv[:, 64:]


def collect(z, states_pieces, heads_rows):
    return pl.pallas_call(
        collect_kernel,
        grid=(1,),
        in_specs=[pl.BlockSpec(memory_space=pltpu.SMEM)]
        + [once(*v.shape) for v in (*states_pieces, heads_rows)],
        out_specs=[once(100, 2240), once(100, 2 * DI), once(100, 82), once(PEERS, 640), once(PEERS, 256)],
        out_shape=[
            jax.ShapeDtypeStruct((100, 2240), F32),
            jax.ShapeDtypeStruct((100, 2 * DI), F32),
            jax.ShapeDtypeStruct((100, 82), F32),
            jax.ShapeDtypeStruct((PEERS, 640), F32),
            jax.ShapeDtypeStruct((PEERS, 256), F32),
        ],
        scratch_shapes=[pltpu.VMEM((PEERS, 104, 640), BF)],
        compiler_params=pltpu.CompilerParams(vmem_limit_bytes=VMEM_LIMIT),
        cost_estimate=pl.CostEstimate(flops=0, bytes_accessed=7_000_000, transcendentals=0),
        name="collect",
    )(z, *states_pieces, heads_rows)


def line_tokens(act, source, x):
    return jnp.concatenate([act[source, lax.rem(x + k, 4)] for k in range(4)], axis=1)


def out_kernel(where_ref, att_ref, mix_ref, w00, w01, w10, w11, *outs):
    att = jnp.zeros((512, WIDTH), F32)
    mix = jnp.zeros((512, WIDTH), F32)
    for a, b, weight in ((0, 0, w00), (0, 1, w01), (1, 0, w10), (1, 1, w11)):
        source = lax.rem(where_ref[0] + a, 2) * 2 + lax.rem(where_ref[2] + b, 2)
        mix = mix + mm(line_tokens(mix_ref, source, where_ref[1]), weight[:LANES, :], 0, 0)
        att = att + mm(line_tokens(att_ref, source, where_ref[1]), weight[LANES:, :], 0, 0)
    for k, ref in ((0, outs[0]), (1, outs[1]), (3, outs[4])):
        ref[:ROWS, :] = att[ROWS * k : ROWS * (k + 1)].astype(BF)
        ref[ROWS:, :] = mix[ROWS * k : ROWS * (k + 1)].astype(BF)
    outs[2][...] = att[2 * ROWS : 3 * ROWS].astype(BF)
    outs[3][...] = mix[2 * ROWS : 3 * ROWS].astype(BF)


def out_projections(where, att, mix, weights):
    two, one = (2 * ROWS, WIDTH), (ROWS, WIDTH)
    shapes = (two, two, one, one, two)
    return pl.pallas_call(
        out_kernel,
        grid=(1,),
        in_specs=[pl.BlockSpec(memory_space=pltpu.SMEM)] + [once(*v.shape) for v in (att, mix, *weights)],
        out_specs=[once(*shape) for shape in shapes],
        out_shape=[jax.ShapeDtypeStruct(shape, BF) for shape in shapes],
        compiler_params=pltpu.CompilerParams(vmem_limit_bytes=VMEM_LIMIT),
        cost_estimate=pl.CostEstimate(
            flops=5_000_000_000, bytes_accessed=10_000_000, transcendentals=0
        ),
        name="out_projections",
    )(where, att, mix, *weights)


def out_back_kernel(where_ref, near, right, far_top, far_low, left, att_ref, mix_ref, w00, w01, w10, w11, *outs):
    d_att_ref, d_mix_ref, *grads = outs
    d_att = jnp.concatenate([near[:ROWS, :], right[:ROWS, :], far_top[...], left[:ROWS, :]], axis=0)
    d_mix = jnp.concatenate([near[ROWS:, :], right[ROWS:, :], far_low[...], left[ROWS:, :]], axis=0)
    x = where_ref[1]
    for a, b, weight, grad in (
        (0, 0, w00, grads[0]),
        (0, 1, w01, grads[1]),
        (1, 0, w10, grads[2]),
        (1, 1, w11, grads[3]),
    ):
        source = lax.rem(where_ref[0] + a, 2) * 2 + lax.rem(where_ref[2] + b, 2)
        d_mix_part = mm(weight[:LANES, :], d_mix, 1, 1).astype(BF)
        d_att_part = mm(weight[LANES:, :], d_att, 1, 1).astype(BF)
        for k in range(4):
            d_mix_ref[source, lax.rem(x + k, 4)] = d_mix_part[:, ROWS * k : ROWS * (k + 1)]
            d_att_ref[source, lax.rem(x + k, 4)] = d_att_part[:, ROWS * k : ROWS * (k + 1)]
        grad_mix = mm(line_tokens(mix_ref, source, x), d_mix)
        grad_att = mm(line_tokens(att_ref, source, x), d_att)
        together = jnp.concatenate([grad_mix, grad_att], axis=0).astype(BF)
        for i in range(8):
            grad[i] = together[OUT_BLOCK * i : OUT_BLOCK * (i + 1)]


def out_projections_back(where, d_proj, att, mix, weights):
    return pl.pallas_call(
        out_back_kernel,
        grid=(1,),
        in_specs=[pl.BlockSpec(memory_space=pltpu.SMEM)]
        + [once(*v.shape) for v in (*d_proj, att, mix, *weights)],
        out_specs=[once(4, 4, 128, ROWS), once(4, 4, LANES, ROWS)] + [once(8, OUT_BLOCK, WIDTH)] * 4,
        out_shape=[
            jax.ShapeDtypeStruct((4, 4, 128, ROWS), BF),
            jax.ShapeDtypeStruct((4, 4, LANES, ROWS), BF),
        ]
        + [jax.ShapeDtypeStruct((8, OUT_BLOCK, WIDTH), BF)] * 4,
        compiler_params=pltpu.CompilerParams(vmem_limit_bytes=VMEM_LIMIT),
        cost_estimate=pl.CostEstimate(
            flops=10_000_000_000, bytes_accessed=20_000_000, transcendentals=0
        ),
        name="out_projections_back",
    )(where, *d_proj, att, mix, *weights)


def halve_kernel(where_ref, kept_ref, came_ref, p0, p1, p2_top, p2_low, p3):
    for k, targets in ((0, (p0, p0)), (1, (p1, p1)), (2, (p2_top, p2_low)), (3, (p3, p3))):
        for h in range(2):
            spot = 4 * h + lax.rem(where_ref[1] + k, 4)
            total = (kept_ref[spot].astype(F32) + came_ref[spot].astype(F32)).astype(BF)
            if k == 2:
                targets[h][...] = total
            else:
                targets[h][ROWS * h : ROWS * (h + 1), :] = total


def halve(where, kept, came):
    two, one = (2 * ROWS, WIDTH), (ROWS, WIDTH)
    shapes = (two, two, one, one, two)
    return pl.pallas_call(
        halve_kernel,
        grid=(1,),
        in_specs=[pl.BlockSpec(memory_space=pltpu.SMEM), once(8, ROWS, WIDTH), once(8, ROWS, WIDTH)],
        out_specs=[once(*shape) for shape in shapes],
        out_shape=[jax.ShapeDtypeStruct(shape, BF) for shape in shapes],
        compiler_params=pltpu.CompilerParams(vmem_limit_bytes=VMEM_LIMIT),
        cost_estimate=pl.CostEstimate(flops=3_000_000, bytes_accessed=10_000_000, transcendentals=0),
        name="halve",
    )(where, kept, came)


def y_parts_kernel(yl_ref, near_0, came_0, near_1, came_1, p0, p1, p2_top, p2_low, p3):
    def total(half, at, count):
        near, came = ((near_0, came_0), (near_1, came_1))[half]
        rows = slice(at, at + count)
        return (near[rows].astype(F32) + came[rows].astype(F32)).astype(BF)

    for yl in range(2):

        @pl.when(yl_ref[0] == yl)
        def _():
            p0[...] = total(0, 4 * yl, 4)
            p1[...] = total(yl, 4 * (1 - yl), 4)
            p2_top[...] = total(1, 4 * yl, 2)
            p2_low[...] = total(1, 4 * yl + 2, 2)
            p3[...] = total(1 - yl, 4 * (1 - yl), 4)


def y_parts(yl, near_0, came_0, near_1, came_1):
    block = near_0.shape[1:]
    shapes = [(count,) + block for count in (4, 4, 2, 2, 4)]
    return pl.pallas_call(
        y_parts_kernel,
        grid=(1,),
        in_specs=[pl.BlockSpec(memory_space=pltpu.SMEM)] + [once(*near_0.shape)] * 4,
        out_specs=[once(*shape) for shape in shapes],
        out_shape=[jax.ShapeDtypeStruct(shape, BF) for shape in shapes],
        compiler_params=pltpu.CompilerParams(vmem_limit_bytes=VMEM_LIMIT),
        cost_estimate=pl.CostEstimate(flops=4_000_000, bytes_accessed=20_000_000, transcendentals=0),
        name="y_parts",
    )(yl, near_0, came_0, near_1, came_1)


def z_parts_kernel(z_ref, *refs):
    ff, out, parts = refs[:3], refs[3:6], refs[6:]

    def total(terms, k):
        at = lax.rem(z_ref[0] + k, 4)
        return sum(term[at].astype(F32) for term in terms)

    for k in range(4):
        empty = jnp.zeros((RING_ROWS - FF_BLOCK - OUT_BLOCK, WIDTH), F32)
        block = jnp.concatenate([total(out, k), total(ff, k), empty], axis=0).astype(BF)
        if k == 2:
            parts[2][...] = block[: RING_ROWS // 2]
            parts[3][...] = block[RING_ROWS // 2 :]
        else:
            parts[(0, 1, 2, 4)[k]][...] = block


def z_parts(z, ff, out):
    one, half = (RING_ROWS, WIDTH), (RING_ROWS // 2, WIDTH)
    shapes = (one, one, half, half, one)
    return pl.pallas_call(
        z_parts_kernel,
        grid=(1,),
        in_specs=[pl.BlockSpec(memory_space=pltpu.SMEM)] + [once(*v.shape) for v in (*ff, *out)],
        out_specs=[once(*shape) for shape in shapes],
        out_shape=[jax.ShapeDtypeStruct(shape, BF) for shape in shapes],
        compiler_params=pltpu.CompilerParams(vmem_limit_bytes=VMEM_LIMIT),
        cost_estimate=pl.CostEstimate(flops=4_000_000, bytes_accessed=10_000_000, transcendentals=0),
        name="z_parts",
    )(z, *ff, *out)


def one_hot(rows, columns, offset, limit=None):
    row = lax.broadcasted_iota(jnp.int32, (rows, columns), 0)
    column = lax.broadcasted_iota(jnp.int32, (rows, columns), 1)
    hit = column == row + offset
    if limit is not None:
        hit = hit & (row < limit)
    return hit.astype(F32).astype(BF)


def head_places(me):
    filled = jnp.where(me == 15, 0, jnp.where(lax.rem(me, 3) == 2, HEAD, 2 * HEAD))
    return 20 * lax.div(me, 3) + 28 * lax.rem(me, 3), filled, 200 - 8 * me


def to_heads_kernel(me_ref, att_0, att_1, att_2, mix_before, mix_own, extra_0, extra_1, out_ref):
    att_at, filled, mix_at = head_places(me_ref[0])
    mix = mm(one_hot(192, 200, mix_at), mix_before[...]) + mm(one_hot(192, 200, mix_at - 200), mix_own[...])
    att = jnp.zeros((128, WIDTH), F32)
    for t, rows in enumerate((att_0, att_1, att_2)):
        att = att + mm(one_hot(128, 100, att_at - 100 * t, filled), rows[...])
    out_ref[:192, :] = mix.astype(BF)
    out_ref[192:256, :] = extra_0[...] + extra_1[...]
    out_ref[256:, :] = att.astype(BF)


def to_heads(me, rows):
    return pl.pallas_call(
        to_heads_kernel,
        grid=(1,),
        in_specs=[pl.BlockSpec(memory_space=pltpu.SMEM)] + [once(*v.shape) for v in rows],
        out_specs=once(384, WIDTH),
        out_shape=jax.ShapeDtypeStruct((384, WIDTH), BF),
        compiler_params=pltpu.CompilerParams(vmem_limit_bytes=VMEM_LIMIT),
        cost_estimate=pl.CostEstimate(flops=600_000_000, bytes_accessed=4_000_000, transcendentals=0),
        name="to_heads",
    )(me, *rows)


def finish_kernel(me_ref, z_ref, *refs):
    pieces, refs = refs[:5], refs[5:]
    gateup_ref, down_ref, att_0, att_1, att_2, mix_before, mix_own, extra_ref, blocks_ref, out_ref = refs
    for spot, block in rep_spots(z_ref, pieces):
        blocks_ref[spot] = block
    for half in range(2):
        for z in range(4):
            block = blocks_ref[2 * z + half].astype(F32)
            i = 4 * half + z
            out_ref[OUT_BLOCK * i : OUT_BLOCK * (i + 1), :] = block[:OUT_BLOCK].astype(BF)
            start, stop = FF_BLOCK * i, min(FF_BLOCK * (i + 1), 3 * FF_ROWS)
            rows = block[OUT_BLOCK : OUT_BLOCK + FF_BLOCK]
            edge = 2 * FF_ROWS
            if start < edge:
                end = min(stop, edge)
                gateup_ref[start:end, :] = rows[: end - start]
            if stop > edge:
                begin = max(start, edge)
                down_ref[begin - edge : stop - edge, :] = rows[begin - start : stop - start]
    att_at, filled, mix_at = head_places(me_ref[0])
    mix, att = out_ref[:192, :], out_ref[256:, :]
    for t, target in enumerate((att_0, att_1, att_2)):
        kept = mm(one_hot(128, 100, att_at - 100 * t, filled), att, 0, 0)
        target[...] = kept.astype(BF)
    mix_before[...] = mm(one_hot(192, 200, mix_at), mix, 0, 0).astype(BF)
    mix_own[...] = mm(one_hot(192, 200, mix_at - 200), mix, 0, 0).astype(BF)
    extra_ref[...] = out_ref[192:256, :]


def finish(me, z, pieces):
    shapes = (
        [((2 * FF_ROWS, WIDTH), F32), ((FF_ROWS, WIDTH), F32)]
        + [((100, WIDTH), BF)] * 3
        + [((200, WIDTH), BF)] * 2
        + [((64, WIDTH), BF)]
    )
    return pl.pallas_call(
        finish_kernel,
        grid=(1,),
        in_specs=[pl.BlockSpec(memory_space=pltpu.SMEM)] * 2 + [once(*v.shape) for v in pieces],
        out_specs=[once(*shape) for shape, _ in shapes],
        out_shape=[jax.ShapeDtypeStruct(shape, kind) for shape, kind in shapes],
        scratch_shapes=[
            pltpu.VMEM((8, RING_ROWS, WIDTH), BF),
            pltpu.VMEM((8 * OUT_BLOCK, WIDTH), BF),
        ],
        compiler_params=pltpu.CompilerParams(vmem_limit_bytes=VMEM_LIMIT),
        cost_estimate=pl.CostEstimate(flops=600_000_000, bytes_accessed=16_000_000, transcendentals=0),
        name="finish",
    )(me, z, *pieces)


def root_norm(values, gain):
    return values * lax.rsqrt(jnp.mean(values * values, axis=-1, keepdims=True) + 1e-06) * gain


def branch_sum(attend_proj, mixer_proj, attend_gain, mixer_gain):
    return root_norm(attend_proj, attend_gain) + root_norm(mixer_proj, mixer_gain)


Y = ("yl", "yh")
SIZES = {"x": 4, "z": 4, "core": 2, "yh": 2, "yl": 2, SHARD: PEERS, Y: 4}


def shift(v, axis, by):
    n, shape = SIZES[axis], v.shape
    if shape[-2] % 16 == 0:
        v = v.reshape(shape[:-2] + (shape[-2] // 16, 16, shape[-1]))
    order = (0, 2, 1, 3) if axis == Y else range(n)
    pairs = [(order[i], order[(i + by) % n]) for i in range(n)]
    return lax.ppermute(v, axis, pairs).reshape(shape)


def gather_x(v, cut=64):
    left = shift(v, "x", 1)
    right = shift(v, "x", -1)
    return [v, right, shift(left[:cut], "x", 1), shift(right[cut:], "x", -1), left]


def add_low(a, b):
    return (a.astype(F32) + b.astype(F32)).astype(BF)


def ring_first(parts, axis):
    p0, p1, top, low, p3 = parts
    cut = top.shape[0]
    top = shift(top, axis, 1)
    low = shift(low, axis, -1)
    ahead = jnp.concatenate([add_low(p1[:cut], top), p1[cut:]], axis=0)
    behind = jnp.concatenate([p3[:cut], add_low(p3[cut:], low)], axis=0)
    return p0, ahead, behind


def ring_second(p0, ahead, behind, axis):
    return p0, shift(ahead, axis, 1), shift(behind, axis, -1)


def total(terms):
    return sum(term.astype(F32) for term in terms)


def reduce_x(parts):
    return total(ring_second(*ring_first(parts, "x"), "x"))


def spread_sum(blocks, axes):
    came = lax.all_to_all(blocks, axes, 0, 0, tiled=False)
    return jnp.sum(came.astype(F32), axis=0).astype(BF)


def rep_gather(v):
    return lax.all_to_all(jnp.broadcast_to(v[None], (8,) + v.shape), REP, 0, 0, tiled=False)


def collect_states(w):
    n = w.shape[0]
    return jnp.concatenate([w[:, :, :3].reshape(n, 48), w[:, :2, 3]], axis=1)


def local(
    tokens,
    segments,
    input_gain,
    attention_weight,
    attend_out,
    mixer_weight,
    param_weight,
    mixer_out,
    attend_gain,
    mixer_gain,
    feed_gain,
    gateup_weight,
    down_weight,
    decay_log,
    step_bias,
    skip_gain,
    cotangent,
):
    me = lax.axis_index(SHARD)
    yh, x, core = lax.axis_index("yh"), lax.axis_index("x"), lax.axis_index("core")
    where = jnp.stack([yh, x, core]).astype(jnp.int32)
    core_word = where[2:]
    me_word = me.astype(jnp.int32)[None]
    yl_word, z_word = (lax.axis_index(name).astype(jnp.int32)[None] for name in ("yl", "z"))
    grouped = (ROWS // 16, 16, WIDTH)
    tok_low, grad_out = tokens.reshape(grouped), cotangent.reshape(grouped)
    tok = tok_low.astype(F32)
    tok_low, grad_out = tok_low.reshape(ROWS, WIDTH), grad_out.reshape(ROWS, WIDTH)

    gains = jnp.concatenate([input_gain, attend_gain, mixer_gain, feed_gain])
    extra = jnp.concatenate(
        [
            jnp.pad(segments.astype(BF), ((0, 0), (0, WIDTH - ROWS))),
            jnp.pad(gains[None], ((0, 0), (0, WIDTH - 400))),
            jnp.zeros((14, WIDTH), BF),
        ],
        axis=0,
    )
    block = jnp.concatenate([tok_low, extra], axis=0)
    far_block = shift(block, "yh", 1)
    left, right = shift(block, "x", 1), shift(block, "x", -1)
    far_block, left, right, attention_weight, mixer_weight, param_weight = lax.optimization_barrier(
        (far_block, left, right, attention_weight, mixer_weight, param_weight)
    )
    far_left, far_right = shift(far_block, "x", 1), shift(far_block, "x", -1)
    blocks = [block, right, shift(left[:64], "x", 1), shift(right[64:], "x", -1), left]
    spread = spread_inputs(attention_weight, mixer_weight, param_weight)
    spread, far_left, far_right, blocks = lax.optimization_barrier((spread, far_left, far_right, blocks))
    blocks += [far_block, far_right, shift(far_left[:64], "x", 1), shift(far_right[64:], "x", -1), far_left]
    weight_in = lax.all_to_all(spread, SHARD, 0, 0, tiled=False).reshape(WIDTH, IN_WIDTH)
    mine = place(where, blocks)
    other = shift(mine, "core", 1)
    low_rows = jnp.stack(in_order(core, mine[:, ROWS : ROWS + 2, :400], other[:, ROWS : ROWS + 2, :400]), axis=1)
    seg = low_rows[:, :, 0, :ROWS].reshape(LENGTH).astype(jnp.int32)
    all_gains = low_rows[:, :, 1].reshape(PEERS, 4, 100).transpose(1, 0, 2)
    gain_in, gain_attend, gain_mixer, gain_feed = all_gains.reshape(4, WIDTH).astype(F32)

    own_attout, own_mixout, _ = lax.optimization_barrier((attend_out, mixer_out, mine))
    own_heads = to_heads(
        me_word,
        (
            own_attout,
            shift(own_attout, SHARD, -1),
            shift(own_attout, SHARD, -2),
            shift(own_mixout, SHARD, 1),
            own_mixout,
            lax.ppermute(own_mixout[72:136], SHARD, [(15, 0)]),
            lax.ppermute(own_mixout[136:200], SHARD, [(15, 1)]),
        ),
    )
    own_heads, weight_in = lax.optimization_barrier((own_heads, weight_in))
    far_heads = shift(own_heads, "yh", 1)
    own_down, own_gateup, _ = lax.optimization_barrier(
        (down_weight, gateup_weight.transpose(1, 2, 0).reshape(2 * FF_ROWS, WIDTH), own_heads)
    )
    far_down, far_gateup = shift(own_down, "yh", 1), shift(own_gateup, "yh", 1)
    normed, projected, kv, kvt = project(core_word, mine, other, gain_in[None], weight_in)
    seg_col, seg_row = seg[:, None], seg[None]
    attended, logs = attend(projected, kv, kvt, seg_col, seg_row)
    attended = lax.all_to_all(attended.reshape(4, 4, 128, ROWS), ("yh", "core"), 0, 0, tiled=False)
    late_grad_out, logs, states_projected = lax.optimization_barrier((grad_out, logs, projected))
    some_grad_out = gather_x(late_grad_out)

    slot_heads = jnp.concatenate([3 * me + jnp.arange(3), jnp.minimum(48 + me, 49)[None]])
    valid = jnp.concatenate([jnp.ones((3,), F32), (me < 2).astype(F32)[None]])
    chunk_segs = seg.reshape(LENGTH // CHUNK, CHUNK)
    last = chunk_segs[:, -1]
    before = jnp.concatenate([last[:1] * 0 - 1, last[:-1]])
    flags = jnp.stack(
        [(chunk_segs == before[:, None]).reshape(-1), (chunk_segs == last[:, None]).reshape(-1)], axis=1
    ).astype(F32)
    par = jnp.pad(jnp.stack([-jnp.exp(decay_log[slot_heads]), step_bias[slot_heads]]), ((0, 0), (0, 4)))
    skip = jnp.repeat(skip_gain[slot_heads], 64)[None]
    state_args = (states_projected, flags, seg_col, seg_row, par, skip)
    mixed, states_y, entries = states(*state_args)
    mixed, attended = lax.optimization_barrier((mixed, attended))
    mixed = lax.all_to_all(mixed.reshape(4, 4, LANES, ROWS), ("yh", "core"), 0, 0, tiled=False)

    mixed, far_heads, far_down, far_gateup = lax.optimization_barrier((mixed, far_heads, far_down, far_gateup))
    out_weights = [own_heads, shift(own_heads, "core", 1), far_heads, shift(far_heads, "core", 1)]
    downs = [own_down, shift(own_down, "core", 1), far_down, shift(far_down, "core", 1)]
    gateups = [own_gateup, shift(own_gateup, "core", 1), far_gateup, shift(far_gateup, "core", 1)]
    both = reduce_x(out_projections(where, attended, mixed, out_weights)).reshape(2, *grouped)
    attend_proj, mixer_proj = both[0], both[1]
    middle = tok + branch_sum(attend_proj, mixer_proj, gain_attend, gain_mixer)
    feed_in = root_norm(middle, gain_feed).astype(BF).reshape(ROWS, WIDTH)

    fed = feed_forward(gather_x(feed_in), some_grad_out, gateups, downs)
    some_feed, some_grad, hidden, d_gate_up = fed[:4]
    out_parts, d_feed_parts = fed[4:9], fed[9:]
    p0, ahead, behind = ring_first(d_feed_parts, "x")
    near_1, far_1 = feed_grads(1, some_feed, some_grad, hidden, d_gate_up)
    ahead, behind, far_1 = lax.optimization_barrier((ahead, behind, far_1))
    d_feed_in = total(ring_second(p0, ahead, behind, "x")).reshape(grouped)
    far_1 = shift(far_1, "core", 1)

    _, feed_pull = jax.vjp(root_norm, middle, gain_feed)
    middle_part, g_feed = feed_pull(d_feed_in)
    d_middle = grad_out.reshape(grouped).astype(F32) + middle_part
    _, branch_pull = jax.vjp(branch_sum, attend_proj, mixer_proj, gain_attend, gain_mixer)
    d_attproj, d_mixproj, g_attend, g_mixer = branch_pull(d_middle)
    d_both = jnp.stack([d_attproj, d_mixproj]).astype(BF).reshape(2 * ROWS, WIDTH)
    left, right = shift(d_both, "x", 1), shift(d_both, "x", -1)
    near_0, far_0 = feed_grads(0, some_feed, some_grad, hidden, d_gate_up)
    left, right, far_0 = lax.optimization_barrier((left, right, far_0))
    d_proj = [d_both, right, shift(left[:ROWS], "x", 1), shift(right[ROWS:], "x", -1), left]
    far_0 = shift(far_0, "core", 1)
    ff_parts = y_parts(yl_word, near_0, far_0, near_1, far_1)
    out_first_x = ring_first(out_parts, "x")
    d_proj, ff_parts, out_first_x = lax.optimization_barrier((d_proj, ff_parts, out_first_x))
    ff_first = ring_first(ff_parts, Y)
    d_attended, d_mixed, out_00, out_01, out_10, out_11 = out_projections_back(
        where, d_proj, attended, mixed, out_weights
    )
    d_mixed = lax.all_to_all(d_mixed, ("yh", "core"), 0, 0, tiled=False).reshape(2, 2, 4, LANES, ROWS)
    d_attended = lax.all_to_all(d_attended, ("yh", "core"), 0, 0, tiled=False).reshape(2, 2, 4, 128, ROWS)

    out_ring = y_parts(yl_word, out_00, shift(out_01, "core", 1), out_10, shift(out_11, "core", 1))

    out_terms_x = ring_second(*out_first_x, "x")
    d_mixed, out_ring, ff_first, out_terms_x = lax.optimization_barrier(
        (d_mixed, out_ring, ff_first, out_terms_x)
    )
    result = (middle + total(out_terms_x).reshape(grouped)).astype(BF)
    ff_terms = ring_second(*ff_first, Y)
    out_first = ring_first(out_ring, Y)
    d_x, d_z, d_bcr, d_par, d_skip = states_back(*state_args, states_y, entries, d_mixed)
    d_x, ff_terms, out_first = lax.optimization_barrier((d_x, ff_terms, out_first))
    heads = jnp.stack([d_par[0, :SLOTS], d_par[1, :SLOTS], d_skip.reshape(SLOTS, 64).sum(axis=1)]) * valid
    heads = jnp.broadcast_to(heads.reshape(1, 3 * SLOTS), (PEERS, 3 * SLOTS))
    small = jnp.concatenate(
        [jnp.pad(g.reshape(PEERS, -1), ((0, 0), (0, 128 - g.size // PEERS))) for g in (g_attend, g_mixer, g_feed, heads)]
        + [jnp.zeros((PEERS, 128), F32)],
        axis=1,
    )
    in_states = in_grads(normed, (d_x, d_z, d_bcr), weight_in[:, 256:], small)
    out_terms = ring_second(*out_first, Y)
    d_attended, in_states, out_terms = lax.optimization_barrier((d_attended, in_states, out_terms))
    in_states = lax.all_to_all(in_states, SHARD, 0, 0, tiled=False)
    first = ring_first(z_parts(z_word, ff_terms, out_terms), "z")
    d_q, d_kv = attend_back(projected, d_attended, kv, kvt, seg_col, seg_row, logs)
    d_q, d_kv, in_states, first = lax.optimization_barrier((d_q, d_kv, in_states, first))
    in_states = spread_sum(in_states.reshape(8, 2, 104, 640), REP)
    terms = ring_second(*first, "z")
    in_heads = in_grads(normed, (d_q, d_kv), weight_in[:, :256], jnp.zeros((PEERS, 256), F32))
    in_states, in_heads, d_q, terms = lax.optimization_barrier((in_states, in_heads, d_q, terms))
    in_heads = lax.all_to_all(in_heads, SHARD, 0, 0, tiled=False)
    yl = yl_word[0]
    rep_block = total(terms).astype(BF)
    pair = jnp.stack(in_order(yl, rep_block, shift(rep_block, "yl", 1)))
    states_pair = jnp.stack(in_order(yl, in_states, shift(in_states, "yl", 1)))

    kept, sent = d_normed_parts(core_word, (d_q, d_kv, d_x, d_z, d_bcr), weight_in)
    line_parts = halve(where, kept, shift(sent, "core", 1))
    in_heads, line_parts, pair, states_pair = lax.optimization_barrier((in_heads, line_parts, pair, states_pair))
    in_heads = spread_sum(in_heads.reshape(8, 2, 104, 256), REP)
    line_first = ring_first(line_parts, "x")
    left, right = shift(pair, "z", 1), shift(pair, "z", -1)
    states_left, states_right = shift(states_pair, "z", 1), shift(states_pair, "z", -1)
    in_heads, line_first, left, right, states_left, states_right = lax.optimization_barrier(
        (in_heads, line_first, left, right, states_left, states_right)
    )
    in_heads = rep_gather(in_heads).reshape(PEERS, 104, 256)
    line_terms = ring_second(*line_first, "x")
    pieces = [pair, right, shift(left[0], "z", 1), shift(right[1], "z", -1), left]
    states_pieces = [
        states_pair,
        states_right,
        shift(states_left[0], "z", 1),
        shift(states_right[1], "z", -1),
        states_left,
    ]
    line_terms, pieces = lax.optimization_barrier((line_terms, pieces))
    sum_gateup, sum_down, *out_rows = finish(me_word, z_word, pieces)
    in_heads, line_terms, out_rows, states_pieces = lax.optimization_barrier(
        (in_heads, line_terms, out_rows, states_pieces)
    )
    att_0, att_1, att_2, mix_before, mix_own, extra = out_rows
    line = total(line_terms)
    line_kept, line_sent = in_order(yh, line[:ROWS], line[ROWS:])
    d_normed = (line_kept + shift(line_sent.astype(BF), "yh", 1)).reshape(grouped)
    _, input_pull = jax.vjp(lambda t: root_norm(t, gain_in), tok)
    grad_tokens = (d_middle + input_pull(d_normed)[0]).astype(BF)

    sum_attention, sum_mixer, sum_param, low_states, low_heads = collect(z_word, states_pieces, in_heads)
    totals = jnp.sum(low_states, axis=0)
    own_in = (totals[512:612] + jnp.sum(low_heads, axis=0)[128:228]) / input_gain.astype(F32)
    g_decay, g_bias, g_skip = collect_states(
        low_states[:, 384 : 384 + 3 * SLOTS].reshape(PEERS, 3, SLOTS).transpose(1, 0, 2)
    )
    sum_gateup = sum_gateup.reshape(2, FF_ROWS, WIDTH).transpose(2, 0, 1)
    sum_attout = total([att_0, shift(att_1, SHARD, 1), shift(att_2, SHARD, 2)])
    extra_0 = jnp.pad(lax.ppermute(extra, SHARD, [(0, 15)]), ((72, 64), (0, 0)))
    extra_1 = jnp.pad(lax.ppermute(extra, SHARD, [(1, 15)]), ((136, 0), (0, 0)))
    sum_mixout = total([mix_own, shift(mix_before, SHARD, -1), extra_0, extra_1])
    return (
        result.reshape(1, ROWS, WIDTH),
        grad_tokens.reshape(1, ROWS, WIDTH),
        own_in,
        sum_attention,
        sum_attout,
        sum_mixer,
        sum_param,
        sum_mixout,
        totals[:100],
        totals[128:228],
        totals[256:356],
        sum_gateup,
        sum_down,
        g_decay,
        g_bias,
        g_skip,
    )


def solution(mesh):
    fine = Mesh(mesh.devices.reshape(4, 2, 2, 4, 2), ("z", "yl", "yh", "x", "core"))
    rows = P(REP, SHARD, None)
    matrix = P(SHARD, None)
    vector = P(SHARD)
    return jax.shard_map(
        local,
        mesh=fine,
        in_specs=(
            rows,
            P(REP, SHARD),
            vector,
            matrix,
            matrix,
            matrix,
            matrix,
            matrix,
            vector,
            vector,
            vector,
            P(None, None, SHARD),
            matrix,
            P(),
            P(),
            P(),
            rows,
        ),
        out_specs=(
            rows,
            rows,
            vector,
            matrix,
            matrix,
            matrix,
            matrix,
            matrix,
            vector,
            vector,
            vector,
            P(None, None, SHARD),
            matrix,
            P(),
            P(),
            P(),
        ),
        check_vma=False,
    )
```

time: 2360 us -> 851 us (0.36)
  waiting for transfers between devices: 1100 us -> 291 us
  blocking collectives: 686 us -> 0 us
  matrix products: 305 us -> 0 us
  Pallas kernels: 0 us -> 276 us
  starting transfers between devices: 9.19 us -> 172 us
  local copies, waits for them, and re-layouts: 112 us -> 53.3 us
  other arithmetic: 111 us -> 52.8 us
    all_gather x10 -> x0, waiting for transfers between devices: 526 us -> none  [the longest x1 192 us: local(): lax.all_gather(gateup_weight, 'shard', axis=2, tiled=True)]
    unnamed x3 -> x0, blocking collectives: 508 us -> none
    unnamed x23 -> x0, waiting for transfers between devices: 503 us -> none
    dot_general x39 -> x0, matrix products: 305 us -> none  [the longest x1 22.5 us: local(): jnp.einsum('tsf,csf->tc', grad_gateup_low, weight_gateup, preferred_eleme...]
    pallas_call x0 -> x22, Pallas kernels: none -> 276 us  [the longest x1 41.9 us: states_back(): pl.pallas_call(state_back_kernel, grid=(STEPS,), in_specs=state_specs(bac...]
    ppermute x0 -> x85, waiting for transfers between devices: none -> 198 us  [the longest x81 161 us: shift(): return lax.ppermute(v, axis, pairs).reshape(shape)]
    ppermute x0 -> x85, starting transfers between devices: none -> 120 us  [the longest x81 114 us: shift(): return lax.ppermute(v, axis, pairs).reshape(shape)]
    psum x2 -> x0, blocking collectives: 97 us -> none  [the longest x1 65.4 us: local(): head_sums = lax.psum((grad_decay, grad_bias, grad_skip), ('rep', 'shard'))]
  transfers between devices with their start and end apart: 19 -> 95, of which waited for: 13 -> 35; matrix products, arithmetic and copies ran while one was open for 31% -> 10% of each run, Pallas kernels for 0% -> 26%
where the time goes in v1:
time: 851 us; the launch traced here: 847 us
  waiting for transfers between devices  291 us (34%)
  Pallas kernels  276 us (32%)
  starting transfers between devices  172 us (20%)
  local copies, waits for them, and re-layouts  53.3 us (6%)
  other arithmetic  52.8 us (6%)
    ppermute x81, waiting for transfers between devices, shift(): return lax.ppermute(v, axis, pairs).reshape(shape)  161 us
    ppermute x81, starting transfers between devices, shift(): return lax.ppermute(v, axis, pairs).reshape(shape)  114 us
    pallas_call x1, Pallas kernels, states_back(): pl.pallas_call(state_back_kernel, grid=(STEPS,), in_specs=state_specs(bac...  41.9 us
    all_to_all x1, waiting for transfers between devices, local(): lax.all_to_all(attended.reshape(4, 4, 128, ROWS), ('yh', 'core'), 0, 0, t...  40.2 us
    all_to_all x2, waiting for transfers between devices, spread_sum(): came = lax.all_to_all(blocks, axes, 0, 0, tiled=False)  37.6 us
    ppermute x1, waiting for transfers between devices, local(): lax.ppermute(own_mixout[72:136], SHARD, [(15, 0)])  37 us
    pallas_call x1, Pallas kernels, feed_forward(): pl.pallas_call(feed_kernel, grid=(1,), in_specs=[once(*v.shape) for v in...  26.9 us
    pallas_call x1, Pallas kernels, attend_back(): pl.pallas_call(attend_back_kernel, grid=(BLOCKS,), in_specs=[pl.BlockSpec...  25.6 us
  transfers between devices with their start and end apart: 95, of which 35 were waited for; matrix products, arithmetic and copies ran while one was open for 10% of the time, Pallas kernels for 26%

profile of v1, /device:TPU:32, one launch (start us, length us, event | category | flops | bytes accessed | tf_op | source)
XLA Modules:
  0.0 847.1 jit_solution(11959048929851160250)
XLA Ops:
  69.3 37.0 %collective-permute-done.13.extra_0 = bf16[64,1600]{1,0:T(8,128)(2,1)} collective-permute-done((bf16[64,1600]{1,0:T(8,128)(2,1)}, bf16[64,1600]{1,0:T(8,128)(2,1)}, u32[]{:S(2)}, u32[]{:S(2)}) %collective-permute-start.13) | collective-permute-done | bytes 204832 | tf_op jit(solution)/shard_map/ppermute | solution.py:1184
  125.8 15.4 %project.1 = (bf16[2048,1600]{1,0:T(8,128)(2,1)}, f32[2048,896]{1,0:T(8,128)}, bf16[2048,128]{1,0:T(8,128)(2,1)}, bf16[128,2048]{1,0:T(8,128)(2,1)}) custom-call(s32[1]{0:T(128)} %bitcast.2.core_ref, bf16[8,144,1600]{2,1,0:T(8,128)(2,1)} %place.1.mine_ref, bf16[8,144,1600]{2,1,0:T(8,128)(2,1)} %bitcast.21.other_ref, f32[1,1600]{1,0:T(1,128)} %unstack.33.gain_ref, ...), custom_call_target="tpu_custom_call" | custom-call | flops 8000000000 | bytes 24000000 | tf_op jit(solution)/shard_map/project/pallas_call | solution.py:539
  141.2 15.5 %attend.1 = (bf16[2,2,4,128,128]{4,3,2,1,0:T(8,128)(2,1)}, f32[8,2048]{1,0:T(8,128)}) custom-call(f32[2048,896]{1,0:T(8,128)} %get-tuple-element.240.q_ref.x_ref.z_ref.bcr_ref, bf16[2048,128]{1,0:T(8,128)(2,1)} %get-tuple-element.237.kv_ref, bf16[128,2048]{1,0:T(8,128)(2,1)} %get-tuple-element.238.kvt_ref, s32[2048,1]{1,0:T(8,128)} %copy.122.key_segs.seg_col, ...), custom_call_target="tpu_custom_call" | custom-call | flops 10000000000 | bytes 4000000 | tf_op jit(solution)/shard_map/attend/pallas_call | solution.py:157
  163.7 23.5 %states.1 = (bf16[2,2,4,256,128]{4,3,2,1,0:T(8,128)(2,1)}, f32[2048,256]{1,0:T(8,128)}, f32[16,16,256]{2,1,0:T(8,128)}) custom-call(f32[2048,896]{1,0:T(8,128)} %get-tuple-element.240.q_ref.x_ref.z_ref.bcr_ref, f32[2048,896]{1,0:T(8,128)} %get-tuple-element.240.q_ref.x_ref.z_ref.bcr_ref, f32[2048,896]{1,0:T(8,128)} %get-tuple-element.240.q_ref.x_ref.z_ref.bcr_ref, ...), custom_call_target="tpu_custom_call" | custom-call | flops 1500000000 | bytes 10000000 | tf_op jit(solution)/shard_map/states/pallas_call | solution.py:396
  187.2 40.2 %all-to-all-done.1.att_ref = bf16[4,4,128,128]{3,2,1,0:T(8,128)(2,1)S(1)} async-done(((bf16[4,4,128,128]{3,2,1,0:T(8,128)(2,1)}), bf16[4,4,128,128]{3,2,1,0:T(8,128)(2,1)S(1)}, u32[]{:S(2)}, u32[]{:S(2)}) %all-to-all-start.1) | async-done | bytes 524320 | tf_op jit(solution)/shard_map/all_to_all | solution.py:1197
  231.4 15.4 %all-to-all-done.2.mix_ref = bf16[4,4,256,128]{3,2,1,0:T(8,128)(2,1)S(1)} async-done(((bf16[4,4,256,128]{3,2,1,0:T(8,128)(2,1)}), bf16[4,4,256,128]{3,2,1,0:T(8,128)(2,1)S(1)}, u32[]{:S(2)}, u32[]{:S(2)}) %all-to-all-start.2) | async-done | bytes 1048608 | tf_op jit(solution)/shard_map/all_to_all | solution.py:1214
  271.9 14.3 %collective-permute-start.23 = (bf16[16,16,1600]{2,1,0:T(8,128)(2,1)S(1)}, bf16[16,16,1600]{2,1,0:T(8,128)(2,1)S(1)}, u32[]{:S(2)}, u32[]{:S(2)}) collective-permute-start(bf16[16,16,1600]{2,1,0:T(8,128)(2,1)S(1)} %bitcast.294), channel_id=1, source_target_pairs={{0,6},{2,0},{4,2},{6,4},{1,7},{3,1},{5,3},{7,5},{8,14},{10,8},{12,... | collective-permute-start | bytes 2457608 | tf_op jit(solution)/shard_map/ppermute | solution.py:1068
  292.4 14.1 %collective-permute-done.23 = bf16[16,16,1600]{2,1,0:T(8,128)(2,1)S(1)} collective-permute-done((bf16[16,16,1600]{2,1,0:T(8,128)(2,1)S(1)}, bf16[16,16,1600]{2,1,0:T(8,128)(2,1)S(1)}, u32[]{:S(2)}, u32[]{:S(2)}) %collective-permute-start.23) | collective-permute-done | bytes 819232 | tf_op jit(solution)/shard_map/ppermute | solution.py:1068
  344.4 26.9 %feed_forward.1 = (bf16[512,1600]{1,0:T(8,128)(2,1)}, bf16[512,1600]{1,0:T(8,128)(2,1)}, bf16[4,512,344]{2,1,0:T(8,128)(2,1)}, bf16[4,512,688]{2,1,0:T(8,128)(2,...) custom-call(bf16[128,1600]{1,0:T(8,128)(2,1)} %multiply_convert_fusi, ...), custom_call_target="tpu_custom_call" | custom-call | flops 24999999488 | bytes 28000000 | tf_op jit(solution)/shard_map/feed_forward/pallas_call | solution.py:605
  374.6 9.7 %feed_grads.2 = (bf16[8,136,1600]{2,1,0:T(8,128)(2,1)}, bf16[8,136,1600]{2,1,0:T(8,128)(2,1)}) custom-call(bf16[512,1600]{1,0:T(8,128)(2,1)} %get-tuple-element.263.feed_ref, bf16[512,1600]{1,0:T(8,128)(2,1)} %get-tuple-element.264.grad_ref, bf16[4,512,344]{2,1,0:T(8,128)(2,1)} %get-tuple-element.265.hidden_ref, ...), custom_call_target="tpu_custom_call" | custom-call | flops 5000000000 | bytes 12000000 | tf_op jit(solution)/shard_map/feed_grads/pallas_call | solution.py:630
  406.6 9.8 %feed_grads.3 = (bf16[8,136,1600]{2,1,0:T(8,128)(2,1)}, bf16[8,136,1600]{2,1,0:T(8,128)(2,1)}) custom-call(bf16[512,1600]{1,0:T(8,128)(2,1)} %get-tuple-element.263.feed_ref, bf16[512,1600]{1,0:T(8,128)(2,1)} %get-tuple-element.264.grad_ref, bf16[4,512,344]{2,1,0:T(8,128)(2,1)} %get-tuple-element.265.hidden_ref, ...), custom_call_target="tpu_custom_call" | custom-call | flops 5000000000 | bytes 12000000 | tf_op jit(solution)/shard_map/feed_grads/pallas_call | solution.py:630
  437.7 9.8 %y_parts.2 = (bf16[4,136,1600]{2,1,0:T(8,128)(2,1)}, bf16[4,136,1600]{2,1,0:T(8,128)(2,1)}, bf16[2,136,1600]{2,1,0:T(8,128)(2,1)}, bf16[2,136,1600]{2,1,0:T(8,128)(2,1)}, bf16[4,136,1600]{2,1,0:T(8,128)(2,1)}) custom-call(s32[1]{0:T(128)} %bitcast.93.yl_ref, bf16[8,136,1600]{2,1,0:T(8,128)(2,1)} %get-tuple-element.273.near_0, ...), custom_call_target="tpu_custom_call" | custom-call | flops 4000000 | bytes 20000000 | tf_op jit(solution)/shard_map/y_parts/pallas_call | solution.py:916
  451.9 13.4 %out_projections_back.1 = (bf16[4,4,128,128]{3,2,1,0:T(8,128)(2,1)}, bf16[4,4,256,128]{3,2,1,0:T(8,128)(2,1)}, bf16[8,48,1600]{2,1,0:T(8,128)(2,1)}, bf16[8,48,1...) custom-call(s32[3]{0:T(128)} %pad_add_fusion.1.where_ref, ...), custom_call_target="tpu_custom_call" | custom-call | flops 10000000000 | bytes 20000000 | tf_op jit(solution)/shard_map/out_projections_back/pallas_call | solution.py:851
  504.2 41.9 %states_back.1 = (bf16[2048,256]{1,0:T(8,128)(2,1)}, bf16[2048,256]{1,0:T(8,128)(2,1)}, bf16[2048,128]{1,0:T(8,128)(2,1)}, f32[2,8]{1,0:T(2,128)}, f32[1,256]{1,0:T(1,128)}) custom-call(f32[2048,896]{1,0:T(8,128)} %get-tuple-element.240.q_ref.x_ref.z_ref.bcr_ref, f32[2048,896]{1,0:T(8,128)} %get-tuple-element.240.q_ref.x_ref.z_ref.bcr_ref, ...), custom_call_target="tpu_custom_call" | custom-call | flops 4000000000 | bytes 12000000 | tf_op jit(solution)/shard_map/states_back/pallas_call | solution.py:421
  555.9 15.2 %in_grads.2 = bf16[16,104,640]{2,1,0:T(8,128)(2,1)} custom-call(bf16[2048,1600]{1,0:T(8,128)(2,1)} %get-tuple-element.314.normed_ref, bf16[2048,256]{1,0:T(8,128)(2,1)} %get-tuple-element.327.refs_0_.x_ref, bf16[2048,256]{1,0:T(8,128)(2,1)} %get-tuple-element.328.refs_1_.z_ref, bf16[2048,128]{1,0:T(8,128)(2,1)} %get-tuple-element.329.refs_2_.bcr_ref, ...), custom_call_target="tpu_custom_call" | custom-call | flops 13107200000 | bytes 14000000 | tf_op jit(solution)/shard_map/in_grads/pallas_call | solution.py:684
  583.7 25.6 %attend_back.1 = (bf16[2048,128]{1,0:T(8,128)(2,1)}, bf16[2048,128]{1,0:T(8,128)(2,1)}) custom-call(f32[2048,896]{1,0:T(8,128)} %get-tuple-element.240.q_ref.x_ref.z_ref.bcr_ref, bf16[2,2,4,128,128]{4,3,2,1,0:T(8,128)(2,1)} %bitcast.109.g_ref, bf16[2048,128]{1,0:T(8,128)(2,1)} %get-tuple-element.237.kv_ref, bf16[128,2048]{1,0:T(8,128)(2,1)} %get-tuple-element.238.kvt_ref, ...), custom_call_target="tpu_custom_call" | custom-call | flops 24999999488 | bytes 5000000 | tf_op jit(solution)/shard_map/attend_back/pallas_call | solution.py:184
  621.8 9.9 %in_grads.3 = bf16[16,104,256]{2,1,0:T(8,128)(2,1)} custom-call(bf16[2048,1600]{1,0:T(8,128)(2,1)} %get-tuple-element.314.normed_ref, bf16[2048,128]{1,0:T(8,128)(2,1)} %get-tuple-element.358.refs_0_.q_ref, bf16[2048,128]{1,0:T(8,128)(2,1)} %get-tuple-element.353.refs_1_.kv_ref, bf16[1600,256]{1,0:T(8,128)(2,1)} %slice.258.refs_2_, ...), custom_call_target="tpu_custom_call" | custom-call | flops 5242880000 | bytes 14000000 | tf_op jit(solution)/shard_map/in_grads/pallas_call | solution.py:684
  631.7 12.1 %all-to-all-done.6 = bf16[8,2,104,640]{3,2,1,0:T(8,128)(2,1)S(1)} async-done(((bf16[8,2,104,640]{3,2,1,0:T(8,128)(2,1)}), bf16[8,2,104,640]{3,2,1,0:T(8,128)(2,1)S(1)}, u32[]{:S(2)}, u32[]{:S(2)}) %all-to-all-start.6) | async-done | bytes 2129952 | tf_op jit(solution)/shard_map/all_to_all | solution.py:1104
  644.8 10.0 %collective-permute-done.62 = bf16[12,16,1600]{2,1,0:T(8,128)(2,1)} collective-permute-done((bf16[12,16,1600]{2,1,0:T(8,128)(2,1)}, bf16[12,16,1600]{2,1,0:T(8,128)(2,1)}, u32[]{:S(2)}, u32[]{:S(2)}) %collective-permute-start.62) | collective-permute-done | bytes 614432 | tf_op jit(solution)/shard_map/ppermute | solution.py:1068
  655.9 13.0 %d_normed.1 = (bf16[8,128,1600]{2,1,0:T(8,128)(2,1)}, bf16[8,128,1600]{2,1,0:T(8,128)(2,1)}) custom-call(s32[1]{0:T(128)} %bitcast.2.core_ref, bf16[2048,128]{1,0:T(8,128)(2,1)} %get-tuple-element.358.refs_0_.q_ref, bf16[2048,128]{1,0:T(8,128)(2,1)} %get-tuple-element.353.refs_1_.kv_ref, bf16[2048,256]{1,0:T(8,128)(2,1)} %get-tuple-element.327.refs_0_.x_ref, ...), custom_call_target="tpu_custom_call" | custom-call | flops 8000000000 | bytes 13000000 | tf_op jit(solution)/shard_map/d_normed/pallas_call | solution.py:710
  681.8 17.1 %collective-permute-done.65 = bf16[12,16,1600]{2,1,0:T(8,128)(2,1)} collective-permute-done((bf16[12,16,1600]{2,1,0:T(8,128)(2,1)S(1)}, bf16[12,16,1600]{2,1,0:T(8,128)(2,1)}, u32[]{:S(2)}, u32[]{:S(2)}) %collective-permute-start.65) | collective-permute-done | bytes 614432 | tf_op jit(solution)/shard_map/ppermute | solution.py:1068
  733.2 25.5 %all-to-all-done.8 = bf16[8,2,104,256]{3,2,1,0:T(8,128)(2,1)S(1)} async-done(((bf16[8,2,104,256]{3,2,1,0:T(8,128)(2,1)}), bf16[8,2,104,256]{3,2,1,0:T(8,128)(2,1)S(1)}, u32[]{:S(2)}, u32[]{:S(2)}) %all-to-all-start.8) | async-done | bytes 852000 | tf_op jit(solution)/shard_map/all_to_all | solution.py:1104
  785.0 10.9 %collective-permute-done.76 = bf16[12,16,1600]{2,1,0:T(8,128)(2,1)} collective-permute-done((bf16[12,16,1600]{2,1,0:T(8,128)(2,1)}, bf16[12,16,1600]{2,1,0:T(8,128)(2,1)}, u32[]{:S(2)}, u32[]{:S(2)}) %collective-permute-start.76) | collective-permute-done | bytes 614432 | tf_op jit(solution)/shard_map/ppermute | solution.py:1068
  820.6 12.4 %collective-permute-done.81 = bf16[100,1600]{1,0:T(8,128)(2,1)} collective-permute-done((bf16[100,1600]{1,0:T(8,128)(2,1)}, bf16[100,1600]{1,0:T(8,128)(2,1)}, u32[]{:S(2)}, u32[]{:S(2)}) %collective-permute-start.81) | collective-permute-done | bytes 320032 | tf_op jit(solution)/shard_map/ppermute | solution.py:1068
  (520 shorter events, 406.1 us)
Async XLA Ops:
  54.3 67.6 %collective-permute-start.9 = (bf16[8,9,16,1600]{3,2,1,0:T(8,128)(2,1)}, bf16[8,9,16,1600]{3,2,1,0:T(8,128)(2,1)}, u32[]{:S(2)}, u32[]{:S(2)}) collective-permute-start(bf16[8,9,16,1600]{3,2,1,0:T(8,128)(2,1)} %bitcast.266), channel_id=1, source_target_pairs={{0,1},{1,0},{2,3},{3,2},{4,5},{5,4},{6,7},{7,6},{8,9},{9,8},{10,11... | collective-permute-start | bytes 11059208 | tf_op jit(solution)/shard_map/ppermute | solution.py:1068
  54.3 61.5 %all-to-all-start = ((bf16[16,100,896]{2,1,0:T(8,128)(2,1)}), bf16[16,100,896]{2,1,0:T(8,128)(2,1)S(1)}, u32[]{:S(2)}, u32[]{:S(2)}) async-start(bf16[16,100,896]{2,1,0:T(8,128)(2,1)} %spread.1), calls=%async_computation | async-start | bytes 5963776 | tf_op jit(solution)/shard_map/all_to_all | solution.py:1167
  58.1 54.1 %collective-permute-start.12 = (bf16[200,1600]{1,0:T(8,128)(2,1)}, bf16[200,1600]{1,0:T(8,128)(2,1)}, u32[]{:S(2)}, u32[]{:S(2)}) collective-permute-start(bf16[200,1600]{1,0:T(8,128)(2,1)} %mix_own), channel_id=1, source_target_pairs={{0,1},{1,2},{2,3},{3,4},{4,5},{5,6},{6,7},{7,8},{8,9},{9,10},{10,1... | collective-permute-start | bytes 1920008 | tf_op jit(solution)/shard_map/ppermute | solution.py:1068
  60.4 45.9 %collective-permute-start.13 = (bf16[64,1600]{1,0:T(8,128)(2,1)}, bf16[64,1600]{1,0:T(8,128)(2,1)}, u32[]{:S(2)}, u32[]{:S(2)}) collective-permute-start(bf16[64,1600]{1,0:T(8,128)(2,1)} %get-tuple-element.529), channel_id=1, source_target_pairs={{15,0},{31,16},{47,32},{63,48},{79,64},{95,80},{111,96},{127,112}} | collective-permute-start | bytes 614408 | tf_op jit(solution)/shard_map/ppermute | solution.py:1184
  62.5 49.7 %collective-permute-start.10 = (bf16[100,1600]{1,0:T(8,128)(2,1)}, bf16[100,1600]{1,0:T(8,128)(2,1)}, u32[]{:S(2)}, u32[]{:S(2)}) collective-permute-start(bf16[100,1600]{1,0:T(8,128)(2,1)} %att_0), channel_id=1, source_target_pairs={{0,15},{1,0},{2,1},{3,2},{4,3},{5,4},{6,5},{7,6},{8,7},{9,8},{10,9... | collective-permute-start | bytes 960008 | tf_op jit(solution)/shard_map/ppermute | solution.py:1068
  69.1 43.1 %collective-permute-start.11 = (bf16[100,1600]{1,0:T(8,128)(2,1)}, bf16[100,1600]{1,0:T(8,128)(2,1)}, u32[]{:S(2)}, u32[]{:S(2)}) collective-permute-start(bf16[100,1600]{1,0:T(8,128)(2,1)} %att_0), channel_id=1, source_target_pairs={{0,14},{1,15},{2,0},{3,1},{4,2},{5,3},{6,4},{7,5},{8,6},{9,7},{10,... | collective-permute-start | bytes 960008 | tf_op jit(solution)/shard_map/ppermute | solution.py:1068
  118.1 113.2 %collective-permute-start.15 = (bf16[24,16,1600]{2,1,0:T(8,128)(2,1)}, bf16[24,16,1600]{2,1,0:T(8,128)(2,1)}, u32[]{:S(2)}, u32[]{:S(2)}) collective-permute-start(bf16[24,16,1600]{2,1,0:T(8,128)(2,1)} %bitcast.277), channel_id=1, source_target_pairs={{0,8},{8,0},{1,9},{9,1},{2,10},{10,2},{3,11},{11,3},{4,12},{12,4},... | collective-permute-start | bytes 3686408 | tf_op jit(solution)/shard_map/ppermute | solution.py:1068
  118.1 113.2 %collective-permute-start.16 = (bf16[344,1600]{1,0:T(8,128)(2,1)}, bf16[344,1600]{1,0:T(8,128)(2,1)}, u32[]{:S(2)}, u32[]{:S(2)}) collective-permute-start(bf16[344,1600]{1,0:T(8,128)(2,1)} %refs_14_), channel_id=1, source_target_pairs={{0,8},{8,0},{1,9},{9,1},{2,10},{10,2},{3,11},{11,3},{4,12},{12,4},... | collective-permute-start | bytes 3302408 | tf_op jit(solution)/shard_map/ppermute | solution.py:1068
  121.7 109.7 %collective-permute-start.17 = (bf16[43,16,1600]{2,1,0:T(8,128)(2,1)}, bf16[43,16,1600]{2,1,0:T(8,128)(2,1)}, u32[]{:S(2)}, u32[]{:S(2)}) collective-permute-start(bf16[43,16,1600]{2,1,0:T(8,128)(2,1)} %bitcast.42), channel_id=1, source_target_pairs={{0,8},{8,0},{1,9},{9,1},{2,10},{10,2},{3,11},{11,3},{4,12},{12,4},... | collective-permute-start | bytes 6604808 | tf_op jit(solution)/shard_map/ppermute | solution.py:1068
  156.8 70.6 %all-to-all-start.1 = ((bf16[4,4,128,128]{3,2,1,0:T(8,128)(2,1)}), bf16[4,4,128,128]{3,2,1,0:T(8,128)(2,1)S(1)}, u32[]{:S(2)}, u32[]{:S(2)}) async-start(bf16[4,4,128,128]{3,2,1,0:T(8,128)(2,1)} %bitcast.300), calls=%async_computation.1 | async-start | bytes 1048576 | tf_op jit(solution)/shard_map/all_to_all | solution.py:1197
  288.8 51.8 %collective-permute-start.32 = (bf16[43,16,1600]{2,1,0:T(8,128)(2,1)}, bf16[43,16,1600]{2,1,0:T(8,128)(2,1)}, u32[]{:S(2)}, u32[]{:S(2)}) collective-permute-start(bf16[43,16,1600]{2,1,0:T(8,128)(2,1)} %bitcast.42), channel_id=1, source_target_pairs={{0,1},{1,0},{2,3},{3,2},{4,5},{5,4},{6,7},{7,6},{8,9},{9,8},{10,11... | collective-permute-start | bytes 6604808 | tf_op jit(solution)/shard_map/ppermute | solution.py:1068
  490.0 81.0 %all-to-all-start.4 = ((bf16[4,4,128,128]{3,2,1,0:T(8,128)(2,1)}), bf16[4,4,128,128]{3,2,1,0:T(8,128)(2,1)}, u32[]{:S(2)}, u32[]{:S(2)}) async-start(bf16[4,4,128,128]{3,2,1,0:T(8,128)(2,1)} %get-tuple-element.313), calls=%async_computation.4 | async-start | bytes 1048576 | tf_op jit(solution)/shard_map/all_to_all | solution.py:1253
  494.2 58.3 %collective-permute-start.54 = (bf16[4,136,1600]{2,1,0:T(8,128)(2,1)}, bf16[4,136,1600]{2,1,0:T(8,128)(2,1)}, u32[]{:S(2)}, u32[]{:S(2)}) collective-permute-start(bf16[4,136,1600]{2,1,0:T(8,128)(2,1)} %pad_maximum_fusion), channel_id=1, source_target_pairs={{0,16},{16,8},{8,24},{24,0},{1,17},{17,9},{9,25},{25,1},{2,18},{18... | collective-permute-start | bytes 5222408 | tf_op jit(solution)/shard_map/ppermute | solution.py:1068
  495.8 56.7 %collective-permute-start.55 = (bf16[4,136,1600]{2,1,0:T(8,128)(2,1)}, bf16[4,136,1600]{2,1,0:T(8,128)(2,1)}, u32[]{:S(2)}, u32[]{:S(2)}) collective-permute-start(bf16[4,136,1600]{2,1,0:T(8,128)(2,1)} %pad_maximum_fusion.1), channel_id=1, source_target_pairs={{0,24},{16,0},{8,16},{24,8},{1,25},{17,1},{9,17},{25,9},{2,26},{18... | collective-permute-start | bytes 5222408 | tf_op jit(solution)/shard_map/ppermute | solution.py:1068
  499.5 50.8 %collective-permute-start.56 = (bf16[2,3,16,1600]{3,2,1,0:T(8,128)(2,1)}, bf16[2,3,16,1600]{3,2,1,0:T(8,128)(2,1)}, u32[]{:S(2)}, u32[]{:S(2)}) collective-permute-start(bf16[2,3,16,1600]{3,2,1,0:T(8,128)(2,1)} %bitcast.110), channel_id=1, source_target_pairs={{0,16},{16,8},{8,24},{24,0},{1,17},{17,9},{9,25},{25,1},{2,18},{18... | collective-permute-start | bytes 921608 | tf_op jit(solution)/shard_map/ppermute | solution.py:1068
  499.6 52.8 %collective-permute-start.57 = (bf16[2,3,16,1600]{3,2,1,0:T(8,128)(2,1)}, bf16[2,3,16,1600]{3,2,1,0:T(8,128)(2,1)S(1)}, u32[]{:S(2)}, u32[]{:S(2)}) collective-permute-start(bf16[2,3,16,1600]{3,2,1,0:T(8,128)(2,1)} %bitcast.112), channel_id=1, source_target_pairs={{0,24},{16,0},{8,16},{24,8},{1,25},{17,1},{9,17},{25,9},{2,26},{18... | collective-permute-start | bytes 921608 | tf_op jit(solution)/shard_map/ppermute | solution.py:1068
  572.1 39.2 %all-to-all-start.5 = ((bf16[16,104,640]{2,1,0:T(8,128)(2,1)}), bf16[16,104,640]{2,1,0:T(8,128)(2,1)}, u32[]{:S(2)}, u32[]{:S(2)}) async-start(bf16[16,104,640]{2,1,0:T(8,128)(2,1)} %in_grads.2), calls=%async_computation.5 | async-start | bytes 4259840 | tf_op jit(solution)/shard_map/all_to_all | solution.py:1276
  707.4 51.4 %collective-permute-start.69 = (bf16[2,12,16,1600]{3,2,1,0:T(8,128)(2,1)S(1)}, bf16[2,12,16,1600]{3,2,1,0:T(8,128)(2,1)}, u32[]{:S(2)}, u32[]{:S(2)}) collective-permute-start(bf16[2,12,16,1600]{3,2,1,0:T(8,128)(2,1)S(1)} %bitcast.263), channel_id=1, source_target_pairs={{0,32},{32,64},{64,96},{96,0},{1,33},{33,65},{65,97},{97,1},{2,34}... | collective-permute-start | bytes 3686408 | tf_op jit(solution)/shard_map/ppermute | solution.py:1068
  708.7 50.2 %collective-permute-start.70 = (bf16[2,12,16,1600]{3,2,1,0:T(8,128)(2,1)S(1)}, bf16[2,12,16,1600]{3,2,1,0:T(8,128)(2,1)}, u32[]{:S(2)}, u32[]{:S(2)}) collective-permute-start(bf16[2,12,16,1600]{3,2,1,0:T(8,128)(2,1)S(1)} %bitcast.264), channel_id=1, source_target_pairs={{0,96},{32,0},{64,32},{96,64},{1,97},{33,1},{65,33},{97,65},{2,98}... | collective-permute-start | bytes 3686408 | tf_op jit(solution)/shard_map/ppermute | solution.py:1068
  709.5 49.3 %collective-permute-start.71 = (bf16[2,2,104,640]{3,2,1,0:T(8,128)(2,1)}, bf16[2,2,104,640]{3,2,1,0:T(8,128)(2,1)}, u32[]{:S(2)}, u32[]{:S(2)}) collective-permute-start(bf16[2,2,104,640]{3,2,1,0:T(8,128)(2,1)} %pad_maximum_fusion.11.refs_0_), channel_id=1, source_target_pairs={{0,32},{32,64},{64,96},{96,0},{1,33},{33,65},{65,97},{97,1},{2,34}... | collective-permute-start | bytes 1597448 | tf_op jit(solution)/shard_map/ppermute | solution.py:1068
  710.7 48.1 %collective-permute-start.72 = (bf16[2,2,104,640]{3,2,1,0:T(8,128)(2,1)}, bf16[2,2,104,640]{3,2,1,0:T(8,128)(2,1)}, u32[]{:S(2)}, u32[]{:S(2)}) collective-permute-start(bf16[2,2,104,640]{3,2,1,0:T(8,128)(2,1)} %pad_maximum_fusion.11.refs_0_), channel_id=1, source_target_pairs={{0,96},{32,0},{64,32},{96,64},{1,97},{33,1},{65,33},{97,65},{2,98}... | collective-permute-start | bytes 1597448 | tf_op jit(solution)/shard_map/ppermute | solution.py:1068
  712.5 46.2 %all-to-all-start.8 = ((bf16[8,2,104,256]{3,2,1,0:T(8,128)(2,1)}), bf16[8,2,104,256]{3,2,1,0:T(8,128)(2,1)S(1)}, u32[]{:S(2)}, u32[]{:S(2)}) async-start(bf16[8,2,104,256]{3,2,1,0:T(8,128)(2,1)} %bitcast.267), calls=%async_computation.8 | async-start | bytes 1703936 | tf_op jit(solution)/shard_map/all_to_all | solution.py:1104
  803.4 41.0 %collective-permute-start.84 = (bf16[64,1600]{1,0:T(8,128)(2,1)}, bf16[64,1600]{1,0:T(8,128)(2,1)}, u32[]{:S(2)}, u32[]{:S(2)}) collective-permute-start(bf16[64,1600]{1,0:T(8,128)(2,1)} %get-tuple-element.419), channel_id=1, source_target_pairs={{1,15},{17,31},{33,47},{49,63},{65,79},{81,95},{97,111},{113,127}} | collective-permute-start | bytes 614408 | tf_op jit(solution)/shard_map/ppermute | solution.py:1331
  804.7 39.6 %collective-permute-start.83 = (bf16[64,1600]{1,0:T(8,128)(2,1)}, bf16[64,1600]{1,0:T(8,128)(2,1)}, u32[]{:S(2)}, u32[]{:S(2)}) collective-permute-start(bf16[64,1600]{1,0:T(8,128)(2,1)} %get-tuple-element.419), channel_id=1, source_target_pairs={{0,15},{16,31},{32,47},{48,63},{64,79},{80,95},{96,111},{112,127}} | collective-permute-start | bytes 614408 | tf_op jit(solution)/shard_map/ppermute | solution.py:1330
  (148 other events, 2163.6 us)

commit v2 on v1

--- a/solution.py
+++ b/solution.py
@@ -926,7 +926,7 @@
 
 
 def z_parts_kernel(z_ref, *refs):
-    ff, out, parts = refs[:3], refs[3:6], refs[6:]
+    ff, out, parts = refs[:3], refs[3:7], refs[7:]
 
     def total(terms, k):
         at = lax.rem(z_ref[0] + k, 4)
@@ -1066,6 +1066,11 @@
     order = (0, 2, 1, 3) if axis == Y else range(n)
     pairs = [(order[i], order[(i + by) % n]) for i in range(n)]
     return lax.ppermute(v, axis, pairs).reshape(shape)
+
+
+def swap_near(v):
+    order, near = (0, 2, 1, 3), (3, 2, 1, 0)
+    return lax.ppermute(v, Y, [(order[i], order[near[i]]) for i in range(4)])
 
 
 def gather_x(v, cut=64):
@@ -1161,10 +1166,16 @@
     )
     far_left, far_right = shift(far_block, "x", 1), shift(far_block, "x", -1)
     blocks = [block, right, shift(left[:64], "x", 1), shift(right[64:], "x", -1), left]
-    spread = spread_inputs(attention_weight, mixer_weight, param_weight)
-    spread, far_left, far_right, blocks = lax.optimization_barrier((spread, far_left, far_right, blocks))
+    spread = spread_inputs(attention_weight, mixer_weight, param_weight).reshape(2, 8, 100, IN_WIDTH)
+    spread_other = swap_near(lax.dynamic_index_in_dim(spread, 1 - yh, 0, keepdims=False))
+    rows_own = lax.dynamic_index_in_dim(spread, yh, 0, keepdims=False)
+    rows_own = lax.all_to_all(rows_own, ("x", "core"), 0, 0, tiled=False)
+    rows_own, spread_other, far_left, far_right, blocks = lax.optimization_barrier(
+        (rows_own, spread_other, far_left, far_right, blocks)
+    )
     blocks += [far_block, far_right, shift(far_left[:64], "x", 1), shift(far_right[64:], "x", -1), far_left]
-    weight_in = lax.all_to_all(spread, SHARD, 0, 0, tiled=False).reshape(WIDTH, IN_WIDTH)
+    rows_other = lax.all_to_all(spread_other, ("x", "core"), 0, 0, tiled=False)
+    weight_in = jnp.stack(in_order(yh, rows_own, rows_other)).reshape(WIDTH, IN_WIDTH)
     mine = place(where, blocks)
     other = shift(mine, "core", 1)
     low_rows = jnp.stack(in_order(core, mine[:, ROWS : ROWS + 2, :400], other[:, ROWS : ROWS + 2, :400]), axis=1)
@@ -1187,15 +1198,20 @@
     )
     own_heads, weight_in = lax.optimization_barrier((own_heads, weight_in))
     far_heads = shift(own_heads, "yh", 1)
-    own_down, own_gateup, _ = lax.optimization_barrier(
-        (down_weight, gateup_weight.transpose(1, 2, 0).reshape(2 * FF_ROWS, WIDTH), own_heads)
-    )
-    far_down, far_gateup = shift(own_down, "yh", 1), shift(own_gateup, "yh", 1)
+    own_gateup, _ = lax.optimization_barrier(
+        (gateup_weight.transpose(1, 2, 0).reshape(2 * FF_ROWS, WIDTH), spread_other)
+    )
+    far_gateup = shift(own_gateup, "yh", 1)
+    own_down, _ = lax.optimization_barrier((down_weight, own_heads))
+    far_down = shift(own_down, "yh", 1)
     normed, projected, kv, kvt = project(core_word, mine, other, gain_in[None], weight_in)
+    kv, far_gateup = lax.optimization_barrier((kv, far_gateup))
     seg_col, seg_row = seg[:, None], seg[None]
     attended, logs = attend(projected, kv, kvt, seg_col, seg_row)
     attended = lax.all_to_all(attended.reshape(4, 4, 128, ROWS), ("yh", "core"), 0, 0, tiled=False)
-    late_grad_out, logs, states_projected = lax.optimization_barrier((grad_out, logs, projected))
+    late_grad_out, far_heads, logs, states_projected = lax.optimization_barrier(
+        (grad_out, far_heads, logs, projected)
+    )
     some_grad_out = gather_x(late_grad_out)
 
     slot_heads = jnp.concatenate([3 * me + jnp.arange(3), jnp.minimum(48 + me, 49)[None]])
@@ -1213,7 +1229,7 @@
     mixed, attended = lax.optimization_barrier((mixed, attended))
     mixed = lax.all_to_all(mixed.reshape(4, 4, LANES, ROWS), ("yh", "core"), 0, 0, tiled=False)
 
-    mixed, far_heads, far_down, far_gateup = lax.optimization_barrier((mixed, far_heads, far_down, far_gateup))
+    mixed, far_down = lax.optimization_barrier((mixed, far_down))
     out_weights = [own_heads, shift(own_heads, "core", 1), far_heads, shift(far_heads, "core", 1)]
     downs = [own_down, shift(own_down, "core", 1), far_down, shift(far_down, "core", 1)]
     gateups = [own_gateup, shift(own_gateup, "core", 1), far_gateup, shift(far_gateup, "core", 1)]
@@ -1260,9 +1276,11 @@
     )
     result = (middle + total(out_terms_x).reshape(grouped)).astype(BF)
     ff_terms = ring_second(*ff_first, Y)
-    out_first = ring_first(out_ring, Y)
+    p0, p1, top, low, p3 = out_ring
+    out_terms = [p0, shift(p1, Y, 1), jnp.concatenate([shift(top, Y, 2), shift(low, Y, 2)]), shift(p3, Y, -1)]
     d_x, d_z, d_bcr, d_par, d_skip = states_back(*state_args, states_y, entries, d_mixed)
-    d_x, ff_terms, out_first = lax.optimization_barrier((d_x, ff_terms, out_first))
+    d_x, ff_terms, out_terms = lax.optimization_barrier((d_x, ff_terms, out_terms))
+    first = ring_first(z_parts(z_word, ff_terms, out_terms), "z")
     heads = jnp.stack([d_par[0, :SLOTS], d_par[1, :SLOTS], d_skip.reshape(SLOTS, 64).sum(axis=1)]) * valid
     heads = jnp.broadcast_to(heads.reshape(1, 3 * SLOTS), (PEERS, 3 * SLOTS))
     small = jnp.concatenate(
@@ -1271,35 +1289,35 @@
         axis=1,
     )
     in_states = in_grads(normed, (d_x, d_z, d_bcr), weight_in[:, 256:], small)
-    out_terms = ring_second(*out_first, Y)
-    d_attended, in_states, out_terms = lax.optimization_barrier((d_attended, in_states, out_terms))
+    d_attended, in_states, first = lax.optimization_barrier((d_attended, in_states, first))
+    terms = ring_second(*first, "z")
     in_states = lax.all_to_all(in_states, SHARD, 0, 0, tiled=False)
-    first = ring_first(z_parts(z_word, ff_terms, out_terms), "z")
     d_q, d_kv = attend_back(projected, d_attended, kv, kvt, seg_col, seg_row, logs)
-    d_q, d_kv, in_states, first = lax.optimization_barrier((d_q, d_kv, in_states, first))
+    d_q, d_kv, in_states, terms = lax.optimization_barrier((d_q, d_kv, in_states, terms))
     in_states = spread_sum(in_states.reshape(8, 2, 104, 640), REP)
-    terms = ring_second(*first, "z")
-    in_heads = in_grads(normed, (d_q, d_kv), weight_in[:, :256], jnp.zeros((PEERS, 256), F32))
-    in_states, in_heads, d_q, terms = lax.optimization_barrier((in_states, in_heads, d_q, terms))
-    in_heads = lax.all_to_all(in_heads, SHARD, 0, 0, tiled=False)
     yl = yl_word[0]
     rep_block = total(terms).astype(BF)
     pair = jnp.stack(in_order(yl, rep_block, shift(rep_block, "yl", 1)))
+    in_heads = in_grads(normed, (d_q, d_kv), weight_in[:, :256], jnp.zeros((PEERS, 256), F32))
+    in_states, in_heads, d_q, pair = lax.optimization_barrier((in_states, in_heads, d_q, pair))
+    left, right = shift(pair, "z", 1), shift(pair, "z", -1)
+    in_heads = lax.all_to_all(in_heads, SHARD, 0, 0, tiled=False)
     states_pair = jnp.stack(in_order(yl, in_states, shift(in_states, "yl", 1)))
 
     kept, sent = d_normed_parts(core_word, (d_q, d_kv, d_x, d_z, d_bcr), weight_in)
     line_parts = halve(where, kept, shift(sent, "core", 1))
-    in_heads, line_parts, pair, states_pair = lax.optimization_barrier((in_heads, line_parts, pair, states_pair))
+    in_heads, line_parts, left, right, states_pair = lax.optimization_barrier(
+        (in_heads, line_parts, left, right, states_pair)
+    )
+    pieces = [pair, right, shift(left[0], "z", 1), shift(right[1], "z", -1), left]
     in_heads = spread_sum(in_heads.reshape(8, 2, 104, 256), REP)
     line_first = ring_first(line_parts, "x")
-    left, right = shift(pair, "z", 1), shift(pair, "z", -1)
     states_left, states_right = shift(states_pair, "z", 1), shift(states_pair, "z", -1)
-    in_heads, line_first, left, right, states_left, states_right = lax.optimization_barrier(
-        (in_heads, line_first, left, right, states_left, states_right)
+    in_heads, line_first, states_left, states_right = lax.optimization_barrier(
+        (in_heads, line_first, states_left, states_right)
     )
     in_heads = rep_gather(in_heads).reshape(PEERS, 104, 256)
     line_terms = ring_second(*line_first, "x")
-    pieces = [pair, right, shift(left[0], "z", 1), shift(right[1], "z", -1), left]
     states_pieces = [
         states_pair,
         states_right,

time: 851 us -> 833 us (0.979)
  waiting for transfers between devices: 291 us -> 268 us
  local copies, waits for them, and re-layouts: 53.3 us -> 63.2 us
    ppermute x81, waiting for transfers between devices: 161 us -> 228 us  [shift(): return lax.ppermute(v, axis, pairs).reshape(shape)]
    all_to_all x1, waiting for transfers between devices: 40.2 us -> 0.01 us  [local(): lax.all_to_all(attended.reshape(4, 4, 128, ROWS), ('yh', 'core'), 0, 0, t...]
    all_to_all x2, waiting for transfers between devices: 37.6 us -> 3.24 us  [spread_sum(): came = lax.all_to_all(blocks, axes, 0, 0, tiled=False)]
    ppermute x1, waiting for transfers between devices: 37 us -> 19.7 us  [local(): lax.ppermute(own_mixout[72:136], SHARD, [(15, 0)])]
  transfers between devices with their start and end apart: 95 -> 97, of which waited for: 35 -> 36; matrix products, arithmetic and copies ran while one was open for 10% -> 10% of each run, Pallas kernels for 26% -> 27%
where the time goes in v2:
time: 833 us; the launch traced here: 826 us
  Pallas kernels  276 us (33%)
  waiting for transfers between devices  268 us (32%)
  starting transfers between devices  166 us (20%)
  local copies, waits for them, and re-layouts  63.2 us (8%)
  other arithmetic  51.2 us (6%)
    ppermute x81, waiting for transfers between devices, shift(): return lax.ppermute(v, axis, pairs).reshape(shape)  228 us
    ppermute x81, starting transfers between devices, shift(): return lax.ppermute(v, axis, pairs).reshape(shape)  105 us
    pallas_call x1, Pallas kernels, states_back(): pl.pallas_call(state_back_kernel, grid=(STEPS,), in_specs=state_specs(bac...  41.9 us
    pallas_call x1, Pallas kernels, feed_forward(): pl.pallas_call(feed_kernel, grid=(1,), in_specs=[once(*v.shape) for v in...  26.5 us
    pallas_call x1, Pallas kernels, attend_back(): pl.pallas_call(attend_back_kernel, grid=(BLOCKS,), in_specs=[pl.BlockSpec...  25.5 us
    pallas_call x2, Pallas kernels, in_grads(): pl.pallas_call(in_grads_kernel, grid=(8,), in_specs=[pl.BlockSpec((256, W...  25.2 us
    pallas_call x1, Pallas kernels, states(): pl.pallas_call(state_kernel, grid=(STEPS,), in_specs=state_specs(lambda i...  23.5 us
    ppermute x1, waiting for transfers between devices, local(): lax.ppermute(own_mixout[72:136], SHARD, [(15, 0)])  19.7 us
  transfers between devices with their start and end apart: 97, of which 36 were waited for; matrix products, arithmetic and copies ran while one was open for 10% of the time, Pallas kernels for 27%

profile of v2, /device:TPU:32, one launch (start us, length us, event | category | flops | bytes accessed | tf_op | source)
XLA Modules:
  0.0 826.5 jit_solution(6898552864990512458)
XLA Ops:
  42.0 27.9 %collective-permute-done.6 = bf16[4,16,1600]{2,1,0:T(8,128)(2,1)S(1)} collective-permute-done((bf16[4,16,1600]{2,1,0:T(8,128)(2,1)S(1)}, bf16[4,16,1600]{2,1,0:T(8,128)(2,1)S(1)}, u32[]{:S(2)}, u32[]{:S(2)}) %collective-permute-start.6) | collective-permute-done | bytes 204832 | tf_op jit(solution)/shard_map/ppermute | solution.py:1068
  105.0 19.7 %collective-permute-done.13.extra_0 = bf16[64,1600]{1,0:T(8,128)(2,1)} collective-permute-done((bf16[64,1600]{1,0:T(8,128)(2,1)}, bf16[64,1600]{1,0:T(8,128)(2,1)}, u32[]{:S(2)}, u32[]{:S(2)}) %collective-permute-start.13) | collective-permute-done | bytes 204832 | tf_op jit(solution)/shard_map/ppermute | solution.py:1195
  150.8 15.4 %project.1 = (bf16[2048,1600]{1,0:T(8,128)(2,1)}, f32[2048,896]{1,0:T(8,128)}, bf16[2048,128]{1,0:T(8,128)(2,1)}, bf16[128,2048]{1,0:T(8,128)(2,1)}) custom-call(s32[1]{0:T(128)} %bitcast.2.core_ref, bf16[8,144,1600]{2,1,0:T(8,128)(2,1)} %place.1.mine_ref, bf16[8,144,1600]{2,1,0:T(8,128)(2,1)} %bitcast.29.other_ref, f32[1,1600]{1,0:T(1,128)} %unstack.33.gain_ref, ...), custom_call_target="tpu_custom_call" | custom-call | flops 8000000000 | bytes 24000000 | tf_op jit(solution)/shard_map/project/pallas_call | solution.py:539
  170.7 15.5 %attend.1 = (bf16[2,2,4,128,128]{4,3,2,1,0:T(8,128)(2,1)}, f32[8,2048]{1,0:T(8,128)}) custom-call(f32[2048,896]{1,0:T(8,128)} %get-tuple-element.244.q_ref.x_ref.z_ref.bcr_ref, bf16[2048,128]{1,0:T(8,128)(2,1)} %get-tuple-element.241.kv_ref, bf16[128,2048]{1,0:T(8,128)(2,1)} %get-tuple-element.242.kvt_ref, s32[2048,1]{1,0:T(8,128)} %copy.150.key_segs.seg_col, ...), custom_call_target="tpu_custom_call" | custom-call | flops 10000000000 | bytes 4000000 | tf_op jit(solution)/shard_map/attend/pallas_call | solution.py:157
  186.3 9.9 %collective-permute-done.15 = bf16[24,16,1600]{2,1,0:T(8,128)(2,1)S(1)} collective-permute-done((bf16[24,16,1600]{2,1,0:T(8,128)(2,1)}, bf16[24,16,1600]{2,1,0:T(8,128)(2,1)S(1)}, u32[]{:S(2)}, u32[]{:S(2)}) %collective-permute-start.15) | collective-permute-done | bytes 1228832 | tf_op jit(solution)/shard_map/ppermute | solution.py:1068
  203.5 23.5 %states.1 = (bf16[2,2,4,256,128]{4,3,2,1,0:T(8,128)(2,1)}, f32[2048,256]{1,0:T(8,128)}, f32[16,16,256]{2,1,0:T(8,128)}) custom-call(f32[2048,896]{1,0:T(8,128)} %get-tuple-element.244.q_ref.x_ref.z_ref.bcr_ref, f32[2048,896]{1,0:T(8,128)} %get-tuple-element.244.q_ref.x_ref.z_ref.bcr_ref, f32[2048,896]{1,0:T(8,128)} %get-tuple-element.244.q_ref.x_ref.z_ref.bcr_ref, ...), custom_call_target="tpu_custom_call" | custom-call | flops 1500000000 | bytes 10000000 | tf_op jit(solution)/shard_map/states/pallas_call | solution.py:396
  230.7 16.0 %all-to-all-done.3.mix_ref = bf16[4,4,256,128]{3,2,1,0:T(8,128)(2,1)S(1)} async-done(((bf16[4,4,256,128]{3,2,1,0:T(8,128)(2,1)}), bf16[4,4,256,128]{3,2,1,0:T(8,128)(2,1)S(1)}, u32[]{:S(2)}, u32[]{:S(2)}) %all-to-all-start.3) | async-done | bytes 1048608 | tf_op jit(solution)/shard_map/all_to_all | solution.py:1230
  282.2 11.8 %collective-permute-done.24 = bf16[16,16,1600]{2,1,0:T(8,128)(2,1)S(1)} collective-permute-done((bf16[16,16,1600]{2,1,0:T(8,128)(2,1)S(1)}, bf16[16,16,1600]{2,1,0:T(8,128)(2,1)S(1)}, u32[]{:S(2)}, u32[]{:S(2)}) %collective-permute-start.24) | collective-permute-done | bytes 819232 | tf_op jit(solution)/shard_map/ppermute | solution.py:1068
  308.5 10.2 %collective-permute-done.25 = bf16[8,16,1600]{2,1,0:T(8,128)(2,1)S(1)} collective-permute-done((bf16[8,16,1600]{2,1,0:T(8,128)(2,1)S(1)}, bf16[8,16,1600]{2,1,0:T(8,128)(2,1)S(1)}, u32[]{:S(2)}, u32[]{:S(2)}) %collective-permute-start.25) | collective-permute-done | bytes 409632 | tf_op jit(solution)/shard_map/ppermute | solution.py:1068
  329.3 8.7 %collective-permute-start.28 = (bf16[4,16,1600]{2,1,0:T(8,128)(2,1)S(1)}, bf16[4,16,1600]{2,1,0:T(8,128)(2,1)S(1)}, u32[]{:S(2)}, u32[]{:S(2)}) collective-permute-start(bf16[4,16,1600]{2,1,0:T(8,128)(2,1)S(1)} %slice.276), channel_id=1, source_target_pairs={{0,6},{2,0},{4,2},{6,4},{1,7},{3,1},{5,3},{7,5},{8,14},{10,8},{12,... | collective-permute-start | bytes 614408 | tf_op jit(solution)/shard_map/ppermute | solution.py:1068
  344.4 26.5 %feed_forward.1 = (bf16[512,1600]{1,0:T(8,128)(2,1)}, bf16[512,1600]{1,0:T(8,128)(2,1)}, bf16[4,512,344]{2,1,0:T(8,128)(2,1)}, bf16[4,512,688]{2,1,0:T(8,128)(2,...) custom-call(bf16[128,1600]{1,0:T(8,128)(2,1)} %multiply_convert_fusi, ...), custom_call_target="tpu_custom_call" | custom-call | flops 24999999488 | bytes 28000000 | tf_op jit(solution)/shard_map/feed_forward/pallas_call | solution.py:605
  374.3 9.7 %feed_grads.2 = (bf16[8,136,1600]{2,1,0:T(8,128)(2,1)}, bf16[8,136,1600]{2,1,0:T(8,128)(2,1)}) custom-call(bf16[512,1600]{1,0:T(8,128)(2,1)} %get-tuple-element.265.feed_ref, bf16[512,1600]{1,0:T(8,128)(2,1)} %get-tuple-element.266.grad_ref, bf16[4,512,344]{2,1,0:T(8,128)(2,1)} %get-tuple-element.267.hidden_ref, ...), custom_call_target="tpu_custom_call" | custom-call | flops 5000000000 | bytes 12000000 | tf_op jit(solution)/shard_map/feed_grads/pallas_call | solution.py:630
  405.7 9.7 %feed_grads.3 = (bf16[8,136,1600]{2,1,0:T(8,128)(2,1)}, bf16[8,136,1600]{2,1,0:T(8,128)(2,1)}) custom-call(bf16[512,1600]{1,0:T(8,128)(2,1)} %get-tuple-element.265.feed_ref, bf16[512,1600]{1,0:T(8,128)(2,1)} %get-tuple-element.266.grad_ref, bf16[4,512,344]{2,1,0:T(8,128)(2,1)} %get-tuple-element.267.hidden_ref, ...), custom_call_target="tpu_custom_call" | custom-call | flops 5000000000 | bytes 12000000 | tf_op jit(solution)/shard_map/feed_grads/pallas_call | solution.py:630
  435.2 9.8 %y_parts.2 = (bf16[4,136,1600]{2,1,0:T(8,128)(2,1)}, bf16[4,136,1600]{2,1,0:T(8,128)(2,1)}, bf16[2,136,1600]{2,1,0:T(8,128)(2,1)}, bf16[2,136,1600]{2,1,0:T(8,128)(2,1)}, bf16[4,136,1600]{2,1,0:T(8,128)(2,1)}) custom-call(s32[1]{0:T(128)} %bitcast.98.yl_ref, bf16[8,136,1600]{2,1,0:T(8,128)(2,1)} %get-tuple-element.275.near_0, ...), custom_call_target="tpu_custom_call" | custom-call | flops 4000000 | bytes 20000000 | tf_op jit(solution)/shard_map/y_parts/pallas_call | solution.py:916
  448.5 13.4 %out_projections_back.1 = (bf16[4,4,128,128]{3,2,1,0:T(8,128)(2,1)}, bf16[4,4,256,128]{3,2,1,0:T(8,128)(2,1)}, bf16[8,48,1600]{2,1,0:T(8,128)(2,1)}, bf16[8,48,1...) custom-call(s32[3]{0:T(128)} %pad_add_fusion.1.where_ref, ...), custom_call_target="tpu_custom_call" | custom-call | flops 10000000000 | bytes 20000000 | tf_op jit(solution)/shard_map/out_projections_back/pallas_call | solution.py:851
  505.1 41.9 %states_back.1 = (bf16[2048,256]{1,0:T(8,128)(2,1)}, bf16[2048,256]{1,0:T(8,128)(2,1)}, bf16[2048,128]{1,0:T(8,128)(2,1)}, f32[2,8]{1,0:T(2,128)}, f32[1,256]{1,0:T(1,128)}) custom-call(f32[2048,896]{1,0:T(8,128)} %get-tuple-element.244.q_ref.x_ref.z_ref.bcr_ref, f32[2048,896]{1,0:T(8,128)} %get-tuple-element.244.q_ref.x_ref.z_ref.bcr_ref, ...), custom_call_target="tpu_custom_call" | custom-call | flops 4000000000 | bytes 12000000 | tf_op jit(solution)/shard_map/states_back/pallas_call | solution.py:421
  569.7 15.3 %in_grads.2 = bf16[16,104,640]{2,1,0:T(8,128)(2,1)} custom-call(bf16[2048,1600]{1,0:T(8,128)(2,1)} %get-tuple-element.316.normed_ref, bf16[2048,256]{1,0:T(8,128)(2,1)} %get-tuple-element.329.refs_0_.x_ref, bf16[2048,256]{1,0:T(8,128)(2,1)} %get-tuple-element.330.refs_1_.z_ref, bf16[2048,128]{1,0:T(8,128)(2,1)} %get-tuple-element.331.refs_2_.bcr_ref, ...), custom_call_target="tpu_custom_call" | custom-call | flops 13107200000 | bytes 14000000 | tf_op jit(solution)/shard_map/in_grads/pallas_call | solution.py:684
  593.6 25.5 %attend_back.1 = (bf16[2048,128]{1,0:T(8,128)(2,1)}, bf16[2048,128]{1,0:T(8,128)(2,1)}) custom-call(f32[2048,896]{1,0:T(8,128)} %get-tuple-element.244.q_ref.x_ref.z_ref.bcr_ref, bf16[2,2,4,128,128]{4,3,2,1,0:T(8,128)(2,1)} %bitcast.114.g_ref, bf16[2048,128]{1,0:T(8,128)(2,1)} %get-tuple-element.241.kv_ref, bf16[128,2048]{1,0:T(8,128)(2,1)} %get-tuple-element.242.kvt_ref, ...), custom_call_target="tpu_custom_call" | custom-call | flops 24999999488 | bytes 5000000 | tf_op jit(solution)/shard_map/attend_back/pallas_call | solution.py:184
  633.5 9.9 %in_grads.3 = bf16[16,104,256]{2,1,0:T(8,128)(2,1)} custom-call(bf16[2048,1600]{1,0:T(8,128)(2,1)} %get-tuple-element.316.normed_ref, bf16[2048,128]{1,0:T(8,128)(2,1)} %get-tuple-element.361.refs_0_.q_ref, bf16[2048,128]{1,0:T(8,128)(2,1)} %get-tuple-element.356.refs_1_.kv_ref, bf16[1600,256]{1,0:T(8,128)(2,1)} %slice.242.refs_2_, ...), custom_call_target="tpu_custom_call" | custom-call | flops 5242880000 | bytes 14000000 | tf_op jit(solution)/shard_map/in_grads/pallas_call | solution.py:684
  643.3 22.0 %collective-permute-done.65 = bf16[12,16,1600]{2,1,0:T(8,128)(2,1)} collective-permute-done((bf16[12,16,1600]{2,1,0:T(8,128)(2,1)}, bf16[12,16,1600]{2,1,0:T(8,128)(2,1)}, u32[]{:S(2)}, u32[]{:S(2)}) %collective-permute-start.65) | collective-permute-done | bytes 614432 | tf_op jit(solution)/shard_map/ppermute | solution.py:1068
  668.9 13.0 %d_normed.1 = (bf16[8,128,1600]{2,1,0:T(8,128)(2,1)}, bf16[8,128,1600]{2,1,0:T(8,128)(2,1)}) custom-call(s32[1]{0:T(128)} %bitcast.2.core_ref, bf16[2048,128]{1,0:T(8,128)(2,1)} %get-tuple-element.361.refs_0_.q_ref, bf16[2048,128]{1,0:T(8,128)(2,1)} %get-tuple-element.356.refs_1_.kv_ref, bf16[2048,256]{1,0:T(8,128)(2,1)} %get-tuple-element.329.refs_0_.x_ref, ...), custom_call_target="tpu_custom_call" | custom-call | flops 8000000000 | bytes 13000000 | tf_op jit(solution)/shard_map/d_normed/pallas_call | solution.py:710
  691.4 16.1 %collective-permute-done.69 = bf16[2,104,640]{2,1,0:T(8,128)(2,1)S(1)} collective-permute-done((bf16[2,104,640]{2,1,0:T(8,128)(2,1)S(1)}, bf16[2,104,640]{2,1,0:T(8,128)(2,1)S(1)}, u32[]{:S(2)}, u32[]{:S(2)}) %collective-permute-start.69) | collective-permute-done | bytes 266272 | tf_op jit(solution)/shard_map/ppermute | solution.py:1068
  760.3 14.4 %collective-permute-done.77 = bf16[12,16,1600]{2,1,0:T(8,128)(2,1)} collective-permute-done((bf16[12,16,1600]{2,1,0:T(8,128)(2,1)}, bf16[12,16,1600]{2,1,0:T(8,128)(2,1)}, u32[]{:S(2)}, u32[]{:S(2)}) %collective-permute-start.77) | collective-permute-done | bytes 614432 | tf_op jit(solution)/shard_map/ppermute | solution.py:1068
  799.3 12.3 %collective-permute-done.82 = bf16[100,1600]{1,0:T(8,128)(2,1)} collective-permute-done((bf16[100,1600]{1,0:T(8,128)(2,1)}, bf16[100,1600]{1,0:T(8,128)(2,1)}, u32[]{:S(2)}, u32[]{:S(2)}) %collective-permute-start.82) | collective-permute-done | bytes 320032 | tf_op jit(solution)/shard_map/ppermute | solution.py:1068
  (526 shorter events, 426.2 us)
Async XLA Ops:
  29.5 42.0 %collective-permute-start.3 = (bf16[8,100,896]{2,0,1:T(8,128)(2,1)}, bf16[8,100,896]{2,0,1:T(8,128)(2,1)S(1)}, u32[]{:S(2)}, u32[]{:S(2)}) collective-permute-start(bf16[8,100,896]{2,0,1:T(8,128)(2,1)} %bitcast.253), channel_id=1, source_target_pairs={{0,24},{16,8},{8,16},{24,0},{1,25},{17,9},{9,17},{25,1},{2,26},{18... | collective-permute-start | bytes 4300808 | tf_op jit(solution)/shard_map/ppermute | solution.py:1073
  30.5 40.9 %all-to-all-start = ((bf16[8,100,896]{2,1,0:T(8,128)(2,1)}), bf16[8,100,896]{2,1,0:T(8,128)(2,1)S(1)}, u32[]{:S(2)}, u32[]{:S(2)}) async-start(bf16[8,100,896]{2,1,0:T(8,128)(2,1)} %get-tuple-element.541), calls=%async_computation | async-start | bytes 2981888 | tf_op jit(solution)/shard_map/all_to_all | solution.py:1172
  88.7 59.6 %collective-permute-start.16 = (bf16[8,9,16,1600]{3,2,1,0:T(8,128)(2,1)}, bf16[8,9,16,1600]{3,2,1,0:T(8,128)(2,1)}, u32[]{:S(2)}, u32[]{:S(2)}) collective-permute-start(bf16[8,9,16,1600]{3,2,1,0:T(8,128)(2,1)} %bitcast.273), channel_id=1, source_target_pairs={{0,1},{1,0},{2,3},{3,2},{4,5},{5,4},{6,7},{7,6},{8,9},{9,8},{10,11... | collective-permute-start | bytes 11059208 | tf_op jit(solution)/shard_map/ppermute | solution.py:1068
  90.0 51.6 %all-to-all-start.1 = ((bf16[8,100,896]{2,1,0:T(8,128)(2,1)}), bf16[8,100,896]{2,1,0:T(8,128)(2,1)S(1)}, u32[]{:S(2)}, u32[]{:S(2)}) async-start(bf16[8,100,896]{2,1,0:T(8,128)(2,1)} %copy.146), calls=%async_computation.1 | async-start | bytes 2981888 | tf_op jit(solution)/shard_map/all_to_all | solution.py:1177
  95.6 41.7 %collective-permute-start.12 = (bf16[200,1600]{1,0:T(8,128)(2,1)}, bf16[200,1600]{1,0:T(8,128)(2,1)}, u32[]{:S(2)}, u32[]{:S(2)}) collective-permute-start(bf16[200,1600]{1,0:T(8,128)(2,1)} %mix_own), channel_id=1, source_target_pairs={{0,1},{1,2},{2,3},{3,4},{4,5},{5,6},{6,7},{7,8},{8,9},{9,10},{10,1... | collective-permute-start | bytes 1920008 | tf_op jit(solution)/shard_map/ppermute | solution.py:1068
  103.3 65.6 %collective-permute-start.17 = (bf16[43,16,1600]{2,1,0:T(8,128)(2,1)}, bf16[43,16,1600]{2,1,0:T(8,128)(2,1)}, u32[]{:S(2)}, u32[]{:S(2)}) collective-permute-start(bf16[43,16,1600]{2,1,0:T(8,128)(2,1)} %bitcast.35), channel_id=1, source_target_pairs={{0,8},{8,0},{1,9},{9,1},{2,10},{10,2},{3,11},{11,3},{4,12},{12,4},... | collective-permute-start | bytes 6604808 | tf_op jit(solution)/shard_map/ppermute | solution.py:1068
  144.6 51.6 %collective-permute-start.15 = (bf16[24,16,1600]{2,1,0:T(8,128)(2,1)}, bf16[24,16,1600]{2,1,0:T(8,128)(2,1)S(1)}, u32[]{:S(2)}, u32[]{:S(2)}) collective-permute-start(bf16[24,16,1600]{2,1,0:T(8,128)(2,1)} %bitcast.282), channel_id=1, source_target_pairs={{0,8},{8,0},{1,9},{9,1},{2,10},{10,2},{3,11},{11,3},{4,12},{12,4},... | collective-permute-start | bytes 3686408 | tf_op jit(solution)/shard_map/ppermute | solution.py:1068
  144.6 102.1 %collective-permute-start.19 = (bf16[24,16,1600]{2,1,0:T(8,128)(2,1)}, bf16[24,16,1600]{2,1,0:T(8,128)(2,1)}, u32[]{:S(2)}, u32[]{:S(2)}) collective-permute-start(bf16[24,16,1600]{2,1,0:T(8,128)(2,1)} %bitcast.283), channel_id=1, source_target_pairs={{0,1},{1,0},{2,3},{3,2},{4,5},{5,4},{6,7},{7,6},{8,9},{9,8},{10,11... | collective-permute-start | bytes 3686408 | tf_op jit(solution)/shard_map/ppermute | solution.py:1068
  144.6 86.1 %collective-permute-start.18 = (bf16[344,1600]{1,0:T(8,128)(2,1)}, bf16[344,1600]{1,0:T(8,128)(2,1)}, u32[]{:S(2)}, u32[]{:S(2)}) collective-permute-start(bf16[344,1600]{1,0:T(8,128)(2,1)} %refs_14_), channel_id=1, source_target_pairs={{0,8},{8,0},{1,9},{9,1},{2,10},{10,2},{3,11},{11,3},{4,12},{12,4},... | collective-permute-start | bytes 3302408 | tf_op jit(solution)/shard_map/ppermute | solution.py:1068
  199.7 47.0 %collective-permute-start.20 = (bf16[24,16,1600]{2,1,0:T(8,128)(2,1)S(1)}, bf16[24,16,1600]{2,1,0:T(8,128)(2,1)}, u32[]{:S(2)}, u32[]{:S(2)}) collective-permute-start(bf16[24,16,1600]{2,1,0:T(8,128)(2,1)S(1)} %collective-permute-done.15), channel_id=1, source_target_pairs={{0,1},{1,0},{2,3},{3,2},{4,5},{5,4},{6,7},{7,6},{8,9},{9,8},{10,11... | collective-permute-start | bytes 3686408 | tf_op jit(solution)/shard_map/ppermute | solution.py:1068
  278.1 43.3 %collective-permute-start.33 = (bf16[43,16,1600]{2,1,0:T(8,128)(2,1)}, bf16[43,16,1600]{2,1,0:T(8,128)(2,1)}, u32[]{:S(2)}, u32[]{:S(2)}) collective-permute-start(bf16[43,16,1600]{2,1,0:T(8,128)(2,1)} %bitcast.35), channel_id=1, source_target_pairs={{0,1},{1,0},{2,3},{3,2},{4,5},{5,4},{6,7},{7,6},{8,9},{9,8},{10,11... | collective-permute-start | bytes 6604808 | tf_op jit(solution)/shard_map/ppermute | solution.py:1068
  278.1 46.2 %collective-permute-start.35 = (bf16[344,1600]{1,0:T(8,128)(2,1)}, bf16[344,1600]{1,0:T(8,128)(2,1)}, u32[]{:S(2)}, u32[]{:S(2)}) collective-permute-start(bf16[344,1600]{1,0:T(8,128)(2,1)} %refs_14_), channel_id=1, source_target_pairs={{0,1},{1,0},{2,3},{3,2},{4,5},{5,4},{6,7},{7,6},{8,9},{9,8},{10,11... | collective-permute-start | bytes 3302408 | tf_op jit(solution)/shard_map/ppermute | solution.py:1068
  300.6 38.3 %collective-permute-start.34 = (bf16[43,16,1600]{2,1,0:T(8,128)(2,1)}, bf16[43,16,1600]{2,1,0:T(8,128)(2,1)}, u32[]{:S(2)}, u32[]{:S(2)}) collective-permute-start(bf16[43,16,1600]{2,1,0:T(8,128)(2,1)} %bitcast.75), channel_id=1, source_target_pairs={{0,1},{1,0},{2,3},{3,2},{4,5},{5,4},{6,7},{7,6},{8,9},{9,8},{10,11... | collective-permute-start | bytes 6604808 | tf_op jit(solution)/shard_map/ppermute | solution.py:1068
  487.4 73.9 %collective-permute-start.55 = (bf16[4,136,1600]{2,1,0:T(8,128)(2,1)}, bf16[4,136,1600]{2,1,0:T(8,128)(2,1)}, u32[]{:S(2)}, u32[]{:S(2)}) collective-permute-start(bf16[4,136,1600]{2,1,0:T(8,128)(2,1)} %pad_maximum_fusion.1), channel_id=1, source_target_pairs={{0,16},{16,8},{8,24},{24,0},{1,17},{17,9},{9,25},{25,1},{2,18},{18... | collective-permute-start | bytes 5222408 | tf_op jit(solution)/shard_map/ppermute | solution.py:1068
  487.5 73.8 %collective-permute-start.56 = (bf16[4,136,1600]{2,1,0:T(8,128)(2,1)}, bf16[4,136,1600]{2,1,0:T(8,128)(2,1)}, u32[]{:S(2)}, u32[]{:S(2)}) collective-permute-start(bf16[4,136,1600]{2,1,0:T(8,128)(2,1)} %pad_maximum_fusion.2), channel_id=1, source_target_pairs={{0,24},{16,0},{8,16},{24,8},{1,25},{17,1},{9,17},{25,9},{2,26},{18... | collective-permute-start | bytes 5222408 | tf_op jit(solution)/shard_map/ppermute | solution.py:1068
  494.6 91.7 %all-to-all-start.5 = ((bf16[4,4,128,128]{3,2,1,0:T(8,128)(2,1)}), bf16[4,4,128,128]{3,2,1,0:T(8,128)(2,1)}, u32[]{:S(2)}, u32[]{:S(2)}) async-start(bf16[4,4,128,128]{3,2,1,0:T(8,128)(2,1)} %get-tuple-element.315), calls=%async_computation.5 | async-start | bytes 1048576 | tf_op jit(solution)/shard_map/all_to_all | solution.py:1269
  498.8 62.5 %collective-permute-start.57 = (bf16[4,3,16,1600]{3,2,1,0:T(8,128)(2,1)}, bf16[4,3,16,1600]{3,2,1,0:T(8,128)(2,1)S(1)}, u32[]{:S(2)}, u32[]{:S(2)}) collective-permute-start(bf16[4,3,16,1600]{3,2,1,0:T(8,128)(2,1)} %bitcast.115), channel_id=1, source_target_pairs={{0,16},{16,8},{8,24},{24,0},{1,17},{17,9},{9,25},{25,1},{2,18},{18... | collective-permute-start | bytes 1843208 | tf_op jit(solution)/shard_map/ppermute | solution.py:1068
  498.8 52.5 %collective-permute-start.59 = (bf16[2,3,16,1600]{3,2,1,0:T(8,128)(2,1)S(1)}, bf16[2,3,16,1600]{3,2,1,0:T(8,128)(2,1)S(1)}, u32[]{:S(2)}, u32[]{:S(2)}) collective-permute-start(bf16[2,3,16,1600]{3,2,1,0:T(8,128)(2,1)S(1)} %bitcast.355), channel_id=1, source_target_pairs={{0,8},{16,24},{8,0},{24,16},{1,9},{17,25},{9,1},{25,17},{2,10},{18... | collective-permute-start | bytes 921608 | tf_op jit(solution)/shard_map/ppermute | solution.py:1068
  502.8 58.5 %collective-permute-start.60 = (bf16[4,3,16,1600]{3,2,1,0:T(8,128)(2,1)}, bf16[4,3,16,1600]{3,2,1,0:T(8,128)(2,1)S(1)}, u32[]{:S(2)}, u32[]{:S(2)}) collective-permute-start(bf16[4,3,16,1600]{3,2,1,0:T(8,128)(2,1)} %bitcast.348), channel_id=1, source_target_pairs={{0,24},{16,0},{8,16},{24,8},{1,25},{17,1},{9,17},{25,9},{2,26},{18... | collective-permute-start | bytes 1843208 | tf_op jit(solution)/shard_map/ppermute | solution.py:1068
  620.4 47.5 %all-to-all-start.7 = ((bf16[8,2,104,640]{3,2,1,0:T(8,128)(2,1)}), bf16[8,2,104,640]{3,2,1,0:T(8,128)(2,1)S(1)}, u32[]{:S(2)}, u32[]{:S(2)}) async-start(bf16[8,2,104,640]{3,2,1,0:T(8,128)(2,1)} %bitcast.134), calls=%async_computation.7 | async-start | bytes 4259840 | tf_op jit(solution)/shard_map/all_to_all | solution.py:1109
  629.3 36.0 %collective-permute-start.65 = (bf16[12,16,1600]{2,1,0:T(8,128)(2,1)}, bf16[12,16,1600]{2,1,0:T(8,128)(2,1)}, u32[]{:S(2)}, u32[]{:S(2)}) collective-permute-start(bf16[12,16,1600]{2,1,0:T(8,128)(2,1)} %bitcast.135), channel_id=1, source_target_pairs={{0,16},{16,0},{1,17},{17,1},{2,18},{18,2},{3,19},{19,3},{4,20},{20... | collective-permute-start | bytes 1843208 | tf_op jit(solution)/shard_map/ppermute | solution.py:1068
  745.1 37.0 %all-to-all-start.10 = ((bf16[8,2,104,256]{3,2,1,0:T(8,128)(2,1)}), bf16[8,2,104,256]{3,2,1,0:T(8,128)(2,1)S(1)}, u32[]{:S(2)}, u32[]{:S(2)}) async-start(bf16[8,2,104,256]{3,2,1,0:T(8,128)(2,1)} %broadcast_in_dim.82), calls=%async_computation.10 | async-start | bytes 1703936 | tf_op jit(solution)/shard_map/all_to_all | solution.py:1114
  782.1 41.7 %collective-permute-start.85 = (bf16[64,1600]{1,0:T(8,128)(2,1)}, bf16[64,1600]{1,0:T(8,128)(2,1)}, u32[]{:S(2)}, u32[]{:S(2)}) collective-permute-start(bf16[64,1600]{1,0:T(8,128)(2,1)} %get-tuple-element.419), channel_id=1, source_target_pairs={{1,15},{17,31},{33,47},{49,63},{65,79},{81,95},{97,111},{113,127}} | collective-permute-start | bytes 614408 | tf_op jit(solution)/shard_map/ppermute | solution.py:1349
  783.4 40.3 %collective-permute-start.84 = (bf16[64,1600]{1,0:T(8,128)(2,1)}, bf16[64,1600]{1,0:T(8,128)(2,1)}, u32[]{:S(2)}, u32[]{:S(2)}) collective-permute-start(bf16[64,1600]{1,0:T(8,128)(2,1)} %get-tuple-element.419), channel_id=1, source_target_pairs={{0,15},{16,31},{32,47},{48,63},{64,79},{80,95},{96,111},{112,127}} | collective-permute-start | bytes 614408 | tf_op jit(solution)/shard_map/ppermute | solution.py:1348
  (151 other events, 2131.1 us)
